TPU v7x, 512 devices: a whole 4x4x16 slice. The times are simulated.
512 devices in a mesh: col: 16 (over x, y), row: 32 (over z, core).
Axes of the slice: x: 4, y: 4, z: 16, core: 2. Of those that a mesh axis runs over, the one named last changes fastest.
Arguments:
- tile_values: bfloat16 [24576, 128, 128], P(('col', 'row')), may hold values from -0.0546875 to 0.0546875
- tile_row: int32 [24576], P(('col', 'row')), may hold values from 0 to 8, as said below
- tile_column: int32 [24576], P(('col', 'row')), may hold values from 0 to 15
- unit_cost: float32 [256, 128], P('col'), may hold values from -5 to 5
- capacity: float32 [256, 128], P('col'), may hold values from 0.3 to 3
- demand: float32 [256, 128, 128], P('row'), may hold values from -6 to 6
- row_kind: int32 [256, 128], P('row'), may hold values 0 or 1
- primal_start: float32 [256, 128, 128], P('col'), may hold values from 0 to 1.5
- dual_start: float32 [256, 128, 128], P('row'), may hold values from -6 to 6
Outputs:
- primal_final: float32 [256, 128, 128], P('col')
- dual_final: float32 [256, 128, 128], P('row')
Inputs may be any that keep to these rules, and one draw needn't show every extreme that they name: The value 8 marks an empty slot; empty slots come after the live ones of a device; the live slots of one device name distinct pairs of tile_row and tile_column.
All inputs are finite; a program needn't handle non-finite values. No bound on the sum of `row_kind` on one device may be relied on, other than what follows from the above.
Results may differ from a plain program's by a relative error of at most 0.004.
Values sent between devices are 32-bit elements; how exact they have to be, the bound alone decides.
A program may use at most 64 MiB of HBM per device.

v0:
```python
import jax
import jax.numpy as jnp
from jax import lax
from jax.sharding import PartitionSpec as P

ITERS = 2


primal_step = 0.5
dual_step = 0.5


def per_device(
    tile_values,
    tile_row,
    tile_column,
    unit_cost,
    capacity,
    demand,
    row_kind,
    primal_start,
    dual_start,
):
    row_blocks = dual_start.shape[0]
    col_blocks = primal_start.shape[0]
    live = tile_row < row_blocks
    row_onehot = (tile_row[:, None] == jnp.arange(row_blocks, dtype=jnp.int32)[None, :]).astype(
        jnp.float32
    )
    col_onehot = (
        (tile_column[:, None] == jnp.arange(col_blocks, dtype=jnp.int32)[None, :]) & live[:, None]
    ).astype(jnp.float32)
    safe_row = jnp.minimum(tile_row, row_blocks - 1)
    cost_full = unit_cost[:, :, None]
    bound_full = capacity[:, :, None]
    primal = primal_start
    dual = dual_start
    for iteration in range(ITERS):
        dual_low = dual.astype(jnp.bfloat16)
        picked = dual_low[safe_row]
        product = jnp.einsum(
            "tij,tis->tjs", tile_values, picked, preferred_element_type=jnp.float32
        )
        partial_adjoint = jnp.einsum("tc,tjs->cjs", col_onehot, product)
        adjoint = lax.psum(partial_adjoint, "row")
        primal_new = jnp.minimum(
            jnp.maximum(primal - primal_step * (cost_full - adjoint), 0.0), bound_full
        )
        extrapolated = (2.0 * primal_new - primal).astype(jnp.bfloat16)
        chosen = extrapolated[tile_column]
        image = jnp.einsum("tij,tjs->tis", tile_values, chosen, preferred_element_type=jnp.float32)
        partial_forward = jnp.einsum("tr,tis->ris", row_onehot, image)
        forward = lax.psum(partial_forward, "col")
        dual_new = dual + dual_step * (demand - forward)
        dual_new = jnp.where(row_kind[:, :, None] == 1, jnp.maximum(dual_new, 0.0), dual_new)
        primal = primal_new
        dual = dual_new
    return (primal, dual)


def solution(mesh):
    placed = (
        P(("col", "row"), None, None),
        P(("col", "row")),
        P(("col", "row")),
        P("col", None),
        P("col", None),
        P("row", None, None),
        P("row", None),
        P("col", None, None),
        P("row", None, None),
    )
    return jax.shard_map(
        per_device,
        mesh=mesh,
        in_specs=placed,
        out_specs=(P("col", None, None), P("row", None, None)),
        check_vma=False,
    )
```

profile of v0, /device:TPU:1, one launch (start us, length us, event | category | flops | bytes accessed | tf_op | source)
XLA Modules:
  0.0 714.3 jit_solution(7020148689712366833)
XLA Ops:
  7.2 0.0 copy-start
  7.2 0.0 all-reduce.5.cloned.1.call-start
  7.2 0.8 broadcast_compare_fusion.1
  8.0 0.7 compare_select_fusion.1
  8.7 1.1 convert_element_type.14
  9.8 0.8 gather_fusion
  10.6 0.0 copy-done.9
  10.6 0.0 copy-done
  10.6 1.9 fusion.22
  12.5 2.0 copy.34
  14.6 0.0 copy-start.6
  14.6 0.0 copy-start.7
  14.6 1.3 fusion.6
  15.9 0.0 all-reduce.5.cloned.1.call-update
  15.9 0.0 all-reduce.7.cloned.1.call-start
  16.0 0.1 copy.21
  16.1 0.1 copy.23
  16.2 215.7 %all-reduce.5.cloned.1.call-done = f32[16,128,128]{2,0,1:T(8,128)} async-done(((f32[16,128,128]{2,0,1:T(8,128)}), f32[16,128,128]{2,0,1:T(8,128)}) %all-reduce.5.cloned.1.call-update) | async-done | bytes 1048592 | tf_op jit(solution)/shard_map/psum | solution.py:45
  231.9 2.5 subtract_convert_fusion.1
  234.4 0.1 copy.26
  234.6 2.0 gather_fusion.1
  236.6 3.8 fusion.23
  240.4 2.0 copy.35
  242.4 0.0 copy-start.10
  242.4 1.1 fusion.4
  243.6 0.0 all-reduce.7.cloned.1.call-update
  243.6 0.0 all-reduce.9.cloned.1.call-start
  243.6 0.1 copy.24
  243.8 114.3 %all-reduce.7.cloned.1.call-done = f32[8,128,128]{2,0,1:T(8,128)} async-done(((f32[8,128,128]{2,0,1:T(8,128)}), f32[8,128,128]{2,0,1:T(8,128)}) %all-reduce.7.cloned.1.call-update) | async-done | bytes 524304 | tf_op jit(solution)/shard_map/psum | solution.py:53
  358.1 2.0 fusion.8
  360.2 1.0 gather_fusion.2
  361.1 1.9 fusion.24
  363.0 2.0 copy.36
  365.1 1.3 fusion.2
  366.4 0.0 all-reduce.9.cloned.1.call-update
  366.4 0.0 all-reduce.11.cloned.1.call-start
  366.5 211.4 %all-reduce.9.cloned.1.call-done = f32[16,128,128]{2,0,1:T(8,128)} async-done(((f32[16,128,128]{2,0,1:T(8,128)}), f32[16,128,128]{2,0,1:T(8,128)}) %all-reduce.9.cloned.1.call-update) | async-done | bytes 1048592 | tf_op jit(solution)/shard_map/psum | solution.py:45
  577.9 3.5 subtract_convert_fusion
  581.3 0.1 copy.30
  581.5 2.1 gather_fusion.3
  583.6 3.8 fusion.25
  587.4 2.0 copy.37
  589.4 1.1 fusion
  590.6 0.0 all-reduce.11.cloned.1.call-update
  590.6 2.6 copy.32
  593.2 111.9 %all-reduce.11.cloned.1.call-done = f32[8,128,128]{2,0,1:T(8,128)} async-done(((f32[8,128,128]{2,0,1:T(8,128)}), f32[8,128,128]{2,0,1:T(8,128)}) %all-reduce.11.cloned.1.call-update) | async-done | bytes 524304 | tf_op jit(solution)/shard_map/psum | solution.py:53
  705.1 1.8 maximum_select_fusion
  706.9 0.9 copy.33
  (33 shorter events, 0.1 us)
Async XLA Ops:
  7.2 3.5 copy-start
  7.2 224.7 %all-reduce.5.cloned.1.call-start = ((), (), s32[]{:S(2)}) async-start(), calls=%async_computation | async-start | bytes 2097152 | tf_op jit(solution)/shard_map/psum | solution.py:45
  8.0 6.6 copy-start.15
  8.7 2.0 copy-start.9
  12.5 2.1 copy-start.11
  14.6 1.4 copy-start.6
  14.6 1.5 copy-start.7
  15.9 216.0 %copy-start.2 = (f32[16,128,128]{2,1,0:T(8,128)S(1)}, f32[16,128,128]{2,1,0:T(8,128)}, u32[]{:S(2)}) copy-start(f32[16,128,128]{2,1,0:T(8,128)} %param.16) | copy-start | bytes 3145732
  15.9 342.2 %all-reduce.7.cloned.1.call-start = ((), (), s32[]{:S(2)}) async-start(), calls=%async_computation.1 | async-start | bytes 1048576 | tf_op jit(solution)/shard_map/psum | solution.py:53
  16.2 218.4 %copy-start.8 = (s32[1024]{0:T(1024)}, s32[1024]{0:T(1024)S(1)}, u32[]{:S(2)}) copy-start(s32[1024]{0:T(1024)S(1)} %pad_clamp_fusion) | copy-start | bytes 12292
  240.4 2.1 copy-start.13
  242.4 1.2 copy-start.10
  243.6 334.3 %all-reduce.9.cloned.1.call-start = ((), (), s32[]{:S(2)}) async-start(), calls=%async_computation.2 | async-start | bytes 2097152 | tf_op jit(solution)/shard_map/psum | solution.py:45
  363.0 2.1 copy-start.12
  363.0 2.1 copy-start.16
  366.4 211.5 %copy-start.3 = (f32[16,128,128]{2,1,0:T(8,128)S(1)}, f32[16,128,128]{2,1,0:T(8,128)}, u32[]{:S(2)}) copy-start(f32[16,128,128]{2,1,0:T(8,128)} %param.16) | copy-start | bytes 3145732
  366.4 338.7 %all-reduce.11.cloned.1.call-start = ((), (), s32[]{:S(2)}) async-start(), calls=%async_computation.3 | async-start | bytes 1048576 | tf_op jit(solution)/shard_map/psum | solution.py:53
  587.4 2.1 copy-start.14
  590.5 114.5 %copy-start.1 = (f32[8,128,128]{2,1,0:T(8,128)S(1)}, f32[8,128,128]{2,1,0:T(8,128)}, u32[]{:S(2)}) copy-start(f32[8,128,128]{2,1,0:T(8,128)} %param.17) | copy-start | bytes 1572868
  590.5 114.5 %copy-start.4 = (f32[8,128,128]{2,1,0:T(8,128)S(1)}, f32[8,128,128]{2,1,0:T(8,128)}, u32[]{:S(2)}) copy-start(f32[8,128,128]{2,1,0:T(8,128)} %param.14) | copy-start | bytes 1572868
  590.5 114.5 %copy-start.5 = (f32[8,128,128]{2,0,1:T(8,128)S(1)}, f32[8,128,128]{2,0,1:T(8,128)}, u32[]{:S(2)}) copy-start(f32[8,128,128]{2,0,1:T(8,128)} %all-reduce.7.cloned.1.call-done) | copy-start | bytes 1572868
Sparse Core Ops, SparseCore 0:
  16.1 215.8 all-reduce.4
  243.7 114.3 all-reduce.6
  366.5 211.2 all-reduce.8
  590.7 114.3 all-reduce.10
where the time goes:
time: 715 us; the launch traced here: 714 us
  waiting for transfers between devices  653 us (91%)
  local copies, waits for them, and re-layouts  18.3 us (3%)
  matrix products  16.1 us (2%)
  between operations  14 us (2%)
  other arithmetic  12.3 us (2%)
    psum x2, waiting for transfers between devices, per_device(): adjoint = lax.psum(partial_adjoint, 'row')  427 us
    psum x2, waiting for transfers between devices, per_device(): forward = lax.psum(partial_forward, 'col')  226 us
  transfers between devices with their start and end apart: 4, of which 4 were waited for; matrix products, arithmetic and copies ran while one was open for 0% of the time, Pallas kernels for 0%

commit v1 on v0

v1 whole, which is shorter than its diff:
```python
import jax
import jax.numpy as jnp
from jax import lax
from jax.experimental import pallas as pl
from jax.experimental.pallas import tpu as pltpu
from jax.sharding import PartitionSpec as P

ITERS = 2
NX, NY, NZ = 4, 4, 16
RB, CB, T, S = 8, 16, 128, 128
H = S // 2
Q = 2
HQ = H // Q
FR = 32
SLOTS = 48

primal_step = 0.5
dual_step = 0.5


def kernel(
    inv_ref,
    tiles,
    cost,
    cap,
    demand,
    kind,
    primal0,
    dual0,
    primal_out,
    dual_out,
    kd,
    pt,
    dt,
    dl,
    ap,
    sib,
    rs_s,
    rs_r,
    fp,
    rx,
    g,
    ry,
    dem,
    ring_send,
    ring_recv,
    sib_send,
    sib_recv,
    f_send,
    f_recv,
):
    col = lax.axis_index("col")
    row = lax.axis_index("row")
    x, y = col // NY, col % NY
    z, core = row // 2, row % 2
    own = pl.multiple_of(core * H, H)
    oth = pl.multiple_of((1 - core) * H, H)

    def zdev(d):
        return (col, ((z + d + NZ) % NZ) * 2 + core)

    sibling = (col, z * 2 + 1 - core)

    def xdev(d):
        return (((x + d) % NX) * NY + y, row)

    def ydev(d):
        return (x * NY + (y + d) % NY, row)

    barrier = pltpu.get_barrier_semaphore()
    peers = [zdev(1), zdev(-1), sibling]
    peers += [xdev(d) for d in (1, 2, 3)] + [ydev(d) for d in (1, 2, 3)]
    for peer in peers:
        pl.semaphore_signal(
            barrier, inc=1, device_id=peer, device_id_type=pl.DeviceIdType.MESH
        )

    def place(p, _):
        idx = inv_ref[p]
        tile = tiles[jnp.maximum(idx, 0)].astype(jnp.float32)
        tile = jnp.where(idx >= 0, tile, 0.0).astype(jnp.bfloat16)
        r0 = pl.multiple_of((p // CB) * T, T)
        kd[p % CB, pl.ds(r0, T), :] = tile
        return 0

    lax.fori_loop(0, RB * CB, place, 0)
    for b in range(RB):
        dt[0, b] = dual0[b].T

    pl.semaphore_wait(barrier, len(peers))

    def remote(src, dst, ss, rs, dev):
        return pltpu.make_async_remote_copy(
            src_ref=src,
            dst_ref=dst,
            send_sem=ss,
            recv_sem=rs,
            device_id=dev,
            device_id_type=pl.DeviceIdType.MESH,
        )

    step_of = (1, -1)

    def rs_copy(it, d, t, q):
        i = (it, d, t - 1, q)
        return remote(
            rs_s.at[i], rs_r.at[i], ring_send.at[it, 0, d, t - 1, q],
            ring_recv.at[it, 0, d, t - 1, q], zdev(step_of[d]),
        )

    def ag_copy(it, d, t, q, c):
        part = pt.at[it + 1, c, pl.ds(own + q * HQ, HQ), :]
        return remote(
            part, part, ring_send.at[it, 1, d, t - 1, q],
            ring_recv.at[it, 1, d, t - 1, q], zdev(step_of[d]),
        )

    def sib_rs(it, c):
        return remote(
            ap.at[it, c, pl.ds(oth, H), :], sib.at[it, c],
            sib_send.at[it, 0, c], sib_recv.at[it, 0, c], sibling,
        )

    def sib_ag(it, c, rows):
        part = pt.at[it + 1, c, pl.ds(rows, H), :]
        return remote(part, part, sib_send.at[it, 1, c], sib_recv.at[it, 1, c], sibling)

    def f_rs1(it, h, d):
        if h == 0:
            dest, dev = (x + d) % NX, xdev(d)
        else:
            dest, dev = (y + d) % NY, ydev(d)
        return remote(
            fp.at[it, pl.ds(2 * dest, 2), pl.ds(h * H, H), :], rx.at[it, h, d - 1],
            f_send.at[it, h, 0, d - 1], f_recv.at[it, h, 0, d - 1], dev,
        )

    def sub(h, k):
        return k // 2, pl.multiple_of((k % 2) * FR, FR)

    def f_rs2(it, h, d):
        if h == 0:
            dest, dev = (y + d) % NY, ydev(d)
        else:
            dest, dev = (x + d) % NX, xdev(d)
        b, s0 = sub(h, dest)
        return remote(
            g.at[it, h, b, pl.ds(s0, FR), :], ry.at[it, h, d - 1],
            f_send.at[it, h, 1, d - 1], f_recv.at[it, h, 1, d - 1], dev,
        )

    outer = (x, y)
    inner = (y, x)

    def f_ag1(it, h, d, k):
        b, s0 = sub(h, k)
        part = dt.at[it + 1, 2 * outer[h] + b, pl.ds(h * H + s0, FR), :]
        return remote(
            part, part, f_send.at[it, h, 2, d - 1], f_recv.at[it, h, 2, d - 1],
            ydev(d) if h == 0 else xdev(d),
        )

    def f_ag2(it, h, d, k):
        part = dt.at[it + 1, pl.ds(2 * k, 2), pl.ds(h * H, H), :]
        return remote(
            part, part, f_send.at[it, h, 3, d - 1], f_recv.at[it, h, 3, d - 1],
            xdev(d) if h == 0 else ydev(d),
        )

    far_first = (2, 1, 3)

    def iteration(it, _):
        for b in range(RB):
            dl[:, b * T : (b + 1) * T] = dt[it, b].astype(jnp.bfloat16)

        def adjoint_block(c):
            ap[it, c] = jnp.dot(dl[...], kd[c], preferred_element_type=jnp.float32)
            sib_rs(it, c).start()

        def dest_right(t):
            return (z + 9 - t) % NZ

        def dest_left(t):
            return (z + 8 + t) % NZ

        def adjoint_pair(t):
            adjoint_block(dest_right(t))
            adjoint_block(dest_left(t))

        def both(c, q):
            return (
                ap[it, c, pl.ds(own + q * HQ, HQ), :]
                + sib[it, c, pl.ds(q * HQ, HQ), :]
            )

        def rs_step(t, first, left):
            cr, cl = dest_right(t), dest_left(t)
            sib_rs(it, cr).wait_recv()
            if left:
                sib_rs(it, cl).wait_recv()
            for q in range(Q):
                value = both(cr, q)
                if not first:
                    rs_copy(it, 0, t - 1, q).wait_recv()
                    value = value + rs_r[it, 0, t - 2, q]
                rs_s[it, 0, t - 1, q] = value
                rs_copy(it, 0, t, q).start()
                if left:
                    value = both(cl, q)
                    if not first:
                        rs_copy(it, 1, t - 1, q).wait_recv()
                        value = value + rs_r[it, 1, t - 2, q]
                    rs_s[it, 1, t - 1, q] = value
                    rs_copy(it, 1, t, q).start()

        def primal_in(t):
            @pl.when(it == 0)
            def _():
                pt[0, 2 * (t - 1)] = primal0[2 * (t - 1)].T
                pt[0, 2 * (t - 1) + 1] = primal0[2 * (t - 1) + 1].T

        adjoint_pair(1)
        adjoint_pair(2)
        rs_step(1, True, True)
        adjoint_pair(3)
        primal_in(1)

        def rs_middle(t, _):
            rs_step(t, False, True)

            @pl.when(t <= 6)
            def _():
                adjoint_pair(t + 2)

            primal_in(t)
            return 0

        lax.fori_loop(2, 8, rs_middle, 0)
        rs_step(8, False, False)
        primal_in(8)

        sib_rs(it, z).wait_recv()
        cost_z = cost[pl.ds(z, 1), :]
        cap_z = cap[pl.ds(z, 1), :]
        for q in range(Q):
            rs_copy(it, 1, 7, q).wait_recv()
            part = both(z, q) + rs_r[it, 1, 6, q]
            rs_copy(it, 0, 8, q).wait_recv()
            adjoint = part + rs_r[it, 0, 7, q]
            rows = pl.ds(own + q * HQ, HQ)
            old = pt[it, z, rows, :]
            new = jnp.minimum(
                jnp.maximum(old - primal_step * (cost_z - adjoint), 0.0), cap_z
            )
            pt[it + 1, z, rows, :] = new
            ag_copy(it, 0, 1, q, z).start()
            ag_copy(it, 1, 1, q, z).start()
        sib_ag(it, z, own).start()

        def image(c):
            ext = (2.0 * pt[it + 1, c] - pt[it, c]).astype(jnp.bfloat16)
            return lax.dot_general(
                ext, kd[c], (((1,), (1,)), ((), ())), preferred_element_type=jnp.float32
            )

        def forward_one(c, first):
            sib_ag(it, c, oth).wait_recv()
            res = image(c)
            for b in range(RB):
                part = res[:, b * T : (b + 1) * T]
                fp[it, b] = part if first else fp[it, b] + part

        def forward_pair(t):
            cr, cl = (z - t + NZ) % NZ, (z + t) % NZ
            sib_ag(it, cr, oth).wait_recv()
            sib_ag(it, cl, oth).wait_recv()
            res = image(cr) + image(cl)
            for b in range(RB):
                fp[it, b] = fp[it, b] + res[:, b * T : (b + 1) * T]

        def ag_step(t, left, right_on, left_on):
            cr, cl = (z - t + NZ) % NZ, (z + t) % NZ
            for q in range(Q):
                ag_copy(it, 0, t, q, cr).wait_recv()
                if right_on:
                    ag_copy(it, 0, t + 1, q, cr).start()
                if left:
                    ag_copy(it, 1, t, q, cl).wait_recv()
                    if left_on:
                        ag_copy(it, 1, t + 1, q, cl).start()
            sib_ag(it, cr, own).start()
            if left:
                sib_ag(it, cl, own).start()

        ag_step(1, True, True, True)
        forward_one(z, True)

        def ag_middle(t, _):
            ag_step(t, True, True, True)
            forward_pair(t - 1)
            return 0

        lax.fori_loop(2, 7, ag_middle, 0)
        ag_step(7, True, True, False)
        forward_pair(6)
        ag_step(8, False, False, False)
        forward_pair(7)
        forward_one((z + 8) % NZ, False)

        for d in far_first:
            f_rs1(it, 0, d).start()
            f_rs1(it, 1, d).start()

        @pl.when(it == 0)
        def _():
            for h in range(2):
                b, _s = sub(h, inner[h])
                dem[h] = demand[2 * outer[h] + b].T

        @pl.when(it == ITERS - 1)
        def _():
            def leave(c, _):
                primal_out[c] = pt[ITERS, c].T
                return 0

            lax.fori_loop(0, CB, leave, 0)

        for h in range(2):
            for d in (1, 2, 3):
                f_rs1(it, h, d).wait_recv()
            rows = pl.ds(h * H, H)
            for b in range(2):
                g[it, h, b] = (
                    fp[it, 2 * outer[h] + b, rows, :]
                    + rx[it, h, 0, b]
                    + rx[it, h, 1, b]
                    + rx[it, h, 2, b]
                )
            for d in far_first:
                f_rs2(it, h, d).start()
        for h in range(2):
            for d in (1, 2, 3):
                f_rs2(it, h, d).wait_recv()
            b, s0 = sub(h, inner[h])
            forward = (
                g[it, h, b, pl.ds(s0, FR), :]
                + ry[it, h, 0]
                + ry[it, h, 1]
                + ry[it, h, 2]
            )
            block = 2 * outer[h] + b
            rows = pl.multiple_of(h * H + s0, FR)
            new = dt[it, block, pl.ds(rows, FR), :] + dual_step * (
                dem[h, pl.ds(rows, FR), :] - forward
            )
            new = jnp.where(
                kind[pl.ds(block, 1), :] == 1, jnp.maximum(new, 0.0), new
            )
            dt[it + 1, block, pl.ds(rows, FR), :] = new
            for d in far_first:
                f_ag1(it, h, d, inner[h]).start()
        for h in range(2):
            for d in (1, 2, 3):
                f_ag1(it, h, d, (inner[h] - d + 4) % 4).wait_recv()
            for d in far_first:
                f_ag2(it, h, d, outer[h]).start()
        for h in range(2):
            for d in (1, 2, 3):
                f_ag2(it, h, d, (outer[h] - d + 4) % 4).wait_recv()
        return 0

    lax.fori_loop(0, ITERS, iteration, 0)
    for b in range(RB):
        dual_out[b] = dt[ITERS, b].T

    def drain(it, _):
        def ring(t, _):
            for q in range(Q):
                rs_copy(it, 0, t, q).wait_send()
                ag_copy(it, 0, t, q, z).wait_send()

                @pl.when(t < 8)
                def _():
                    rs_copy(it, 1, t, q).wait_send()
                    ag_copy(it, 1, t, q, z).wait_send()

            return 0

        lax.fori_loop(1, 9, ring, 0)

        def blocks(c, _):
            sib_rs(it, c).wait_send()
            sib_ag(it, c, own).wait_send()
            return 0

        lax.fori_loop(0, CB, blocks, 0)
        for h in range(2):
            for d in (1, 2, 3):
                f_rs1(it, h, d).wait_send()
                f_rs2(it, h, d).wait_send()
                f_ag1(it, h, d, inner[h]).wait_send()
                f_ag2(it, h, d, outer[h]).wait_send()
        return 0

    lax.fori_loop(0, ITERS, drain, 0)


def per_device(
    tile_values,
    tile_row,
    tile_column,
    unit_cost,
    capacity,
    demand,
    row_kind,
    primal_start,
    dual_start,
):
    place = jnp.where(tile_row < RB, tile_row * CB + tile_column, RB * CB)
    slot = jnp.arange(SLOTS, dtype=jnp.int32)
    hit = place[:, None] == jnp.arange(RB * CB, dtype=jnp.int32)[None, :]
    inv = jnp.max(jnp.where(hit, slot[:, None], -1), axis=0)
    vmem = pl.BlockSpec(memory_space=pltpu.VMEM)
    f32, bf16 = jnp.float32, jnp.bfloat16
    dma = pltpu.SemaphoreType.DMA
    return pl.pallas_call(
        kernel,
        out_shape=(
            jax.ShapeDtypeStruct((CB, T, S), f32),
            jax.ShapeDtypeStruct((RB, T, S), f32),
        ),
        in_specs=[pl.BlockSpec(memory_space=pltpu.SMEM)] + [vmem] * 7,
        out_specs=(vmem, vmem),
        scratch_shapes=[
            pltpu.VMEM((CB, RB * T, T), bf16),
            pltpu.VMEM((ITERS + 1, CB, S, T), f32),
            pltpu.VMEM((ITERS + 1, RB, S, T), f32),
            pltpu.VMEM((S, RB * T), bf16),
            pltpu.VMEM((ITERS, CB, S, T), f32),
            pltpu.VMEM((ITERS, CB, H, T), f32),
            pltpu.VMEM((ITERS, 2, 8, Q, HQ, T), f32),
            pltpu.VMEM((ITERS, 2, 8, Q, HQ, T), f32),
            pltpu.VMEM((ITERS, RB, S, T), f32),
            pltpu.VMEM((ITERS, 2, 3, 2, H, T), f32),
            pltpu.VMEM((ITERS, 2, 2, H, T), f32),
            pltpu.VMEM((ITERS, 2, 3, FR, T), f32),
            pltpu.VMEM((2, S, T), f32),
            dma((ITERS, 2, 2, 8, Q)),
            dma((ITERS, 2, 2, 8, Q)),
            dma((ITERS, 2, CB)),
            dma((ITERS, 2, CB)),
            dma((ITERS, 2, 4, 3)),
            dma((ITERS, 2, 4, 3)),
        ],
        compiler_params=pltpu.CompilerParams(
            collective_id=0, has_side_effects=True, vmem_limit_bytes=48 << 20
        ),
        cost_estimate=pl.CostEstimate(
            flops=8 * SLOTS * T * T * S, bytes_accessed=6 << 20, transcendentals=0
        ),
    )(
        inv,
        tile_values,
        unit_cost,
        capacity,
        demand,
        row_kind,
        primal_start,
        dual_start,
    )


def solution(mesh):
    placed = (
        P(("col", "row"), None, None),
        P(("col", "row")),
        P(("col", "row")),
        P("col", None),
        P("col", None),
        P("row", None, None),
        P("row", None),
        P("col", None, None),
        P("row", None, None),
    )
    return jax.shard_map(
        per_device,
        mesh=mesh,
        in_specs=placed,
        out_specs=(P("col", None, None), P("row", None, None)),
        check_vma=False,
    )
```

time: 715 us -> 161 us (0.23)
  waiting for transfers between devices: 653 us -> 0 us
  Pallas kernels: 0 us -> 150 us
  matrix products: 16.1 us -> 0 us
  between operations: 14 us -> 0.65 us
  other arithmetic: 12.3 us -> 0.77 us
  local copies, waits for them, and re-layouts: 18.3 us -> 8.55 us
    psum x4 -> x0, waiting for transfers between devices: 653 us -> none  [the longest x2 427 us: per_device(): adjoint = lax.psum(partial_adjoint, 'row')]
    pallas_call x0 -> x1, Pallas kernels: none -> 150 us  [per_device(): pl.pallas_call(kernel, out_shape=(jax.ShapeDtypeStruct((CB, T, S), f32),...]
    dot_general x8 -> x0, matrix products: 16.1 us -> none  [the longest x2 7.58 us: per_device(): jnp.einsum('tij,tjs->tis', tile_values, chosen, preferred_element_type=jn...]
    convert_element_type x4 -> x0, other arithmetic: 9.13 us -> none  [the longest x2 6.03 us: per_device(): extrapolated = (2.0 * primal_new - primal).astype(jnp.bfloat16)]
    dot_general x4 -> x0, local copies, waits for them, and re-layouts: 8.16 us -> none  [the longest x2 4.08 us: per_device(): jnp.einsum('tij,tis->tjs', tile_values, picked, preferred_element_type=jn...]
  transfers between devices with their start and end apart: 4 -> 0, of which waited for: 4 -> 0; matrix products, arithmetic and copies ran while one was open for 0% -> 0% of each run, Pallas kernels for 0% -> 0%
where the time goes in v1:
time: 161 us; the launch traced here: 160 us
  Pallas kernels  150 us (93%)
  local copies, waits for them, and re-layouts  8.55 us (5%)
    pallas_call x1, Pallas kernels, per_device(): pl.pallas_call(kernel, out_shape=(jax.ShapeDtypeStruct((CB, T, S), f32),...  150 us
    unnamed x16, local copies, waits for them, and re-layouts  8.55 us

profile of v1, /device:TPU:1, one launch (start us, length us, event | category | flops | bytes accessed | tf_op | source)
XLA Modules:
  0.0 159.9 jit_solution(17960324132841295589)
XLA Ops:
  0.6 0.7 compare_select_fusion
  1.3 0.1 select_reduce_fusion.inv_ref
  1.4 0.0 copy-start
  1.4 1.4 copy-done
  2.8 0.0 copy-start.1
  2.8 1.2 copy-done.1
  4.0 0.0 copy-start.2
  4.0 1.0 copy-done.2
  5.1 0.0 copy-start.3
  5.1 1.0 copy-done.3
  6.1 0.0 copy-start.4
  6.1 0.7 copy-done.4
  6.8 0.0 copy-start.5
  6.8 0.7 copy-done.5
  7.5 0.0 copy-start.6
  7.5 0.7 copy-done.6
  8.2 149.9 %shard_map.104 = (f32[16,128,128]{2,1,0:T(8,128)S(1)}, f32[8,128,128]{2,1,0:T(8,128)S(1)}) custom-call(s32[128]{0:T(128)S(1)} %select_reduce_fusion.inv_ref, bf16[48,128,128]{2,1,0:T(8,128)(2,1)S(1)} %copy-done, f32[16,128]{1,0:T(8,128)S(1)} %copy-done.4, f32[16,128]{1,0:T(8,128)S(1)} %copy-done.5, f32[8,128,128]{2,1,0:T(8,128)S(1)} %copy-done.2, ...), custom_call_target="tpu_custom_call" | custom-call | flops 805306368 | bytes 6291456 | tf_op jit(solution)/shard_map/pallas_call | solution.py:426
  158.2 1.0 copy.13
  159.1 0.8 copy.14
Async XLA Ops:
  1.4 1.4 copy-start
  2.8 1.2 copy-start.1
  4.0 1.0 copy-start.2
  5.1 1.0 copy-start.3
  6.1 0.7 copy-start.4
  6.8 0.7 copy-start.5
  7.5 0.7 copy-start.6

commit v2 on v1

v2 whole, which is shorter than its diff:
```python
import jax
import jax.numpy as jnp
from jax import lax
from jax.experimental import pallas as pl
from jax.experimental.pallas import tpu as pltpu
from jax.sharding import PartitionSpec as P

ITERS = 2
NX, NY, NZ = 4, 4, 16
RB, CB, T, S = 8, 16, 128, 128
H = S // 2
FR = 32
SLOTS = 48

PARENT = {1: 0, 4: 0, 2: 1, 5: 4, 7: 4, 3: 2, 6: 5, 8: 7}
LEVELS = ((0,), (4, 1), (7, 5, 2), (8, 6, 3))
OFFS = (0, 1, -1, 4, -4, 2, -2, 5, -5, 7, -7, 3, -3, 6, -6, 8)
POS = {o: p for p, o in enumerate(OFFS)}
POS[-8] = POS[8]
GROUPS = ((0, 1), (1, 5), (5, 11), (11, 16))
HOPS = sorted({s * (d - u) for d, u in PARENT.items() for s in (1, -1)})

primal_step = 0.5
dual_step = 0.5


def children(d):
    return [c for c, u in PARENT.items() if u == d]


def half(s, d):
    if d == 8:
        return (0 if s == 1 else H // 2), H // 2
    return 0, H


def kernel(
    inv_ref,
    tiles_hbm,
    cost_hbm,
    cap_hbm,
    demand_hbm,
    kind_hbm,
    primal_hbm,
    dual_hbm,
    primal_out,
    dual_out,
    tiles,
    cost,
    cap,
    kind,
    primal0,
    dual0,
    dem0,
    kd,
    pt,
    dt,
    dl,
    ext,
    ap,
    sib,
    rs_s,
    rs_r,
    fp,
    rx,
    g,
    ry,
    dem,
    local_sem,
    ring_send,
    ring_recv,
    sib_send,
    sib_recv,
    f_send,
    f_recv,
):
    col = lax.axis_index("col")
    row = lax.axis_index("row")
    x, y = col // NY, col % NY
    z, core = row // 2, row % 2
    own = pl.multiple_of(core * H, H)
    oth = pl.multiple_of((1 - core) * H, H)
    outer = (x, y)
    inner = (y, x)

    def block_at(p):
        return (z + OFFS[p] + NZ) % NZ

    def zdev(d):
        return (col, ((z + d + NZ) % NZ) * 2 + core)

    sibling = (col, z * 2 + 1 - core)

    def xdev(d):
        return (((x + d) % NX) * NY + y, row)

    def ydev(d):
        return (x * NY + (y + d) % NY, row)

    def sub(h, k):
        return k // 2, pl.multiple_of((k % 2) * FR, FR)

    dem_block = [2 * outer[h] + sub(h, inner[h])[0] for h in range(2)]
    loads = [
        pltpu.make_async_copy(src, dst, local_sem.at[n])
        for n, (src, dst) in enumerate(
            [
                (dual_hbm, dual0),
                (tiles_hbm, tiles),
                (primal_hbm, primal0),
                (cost_hbm, cost),
                (cap_hbm, cap),
                (kind_hbm, kind),
                (demand_hbm.at[dem_block[0]], dem0.at[0]),
                (demand_hbm.at[dem_block[1]], dem0.at[1]),
            ]
        )
    ]
    for load in loads:
        load.start()

    barrier = pltpu.get_barrier_semaphore()
    peers = [zdev(d) for d in HOPS] + [sibling]
    peers += [xdev(d) for d in (1, 2, 3)] + [ydev(d) for d in (1, 2, 3)]
    for peer in peers:
        pl.semaphore_signal(
            barrier, inc=1, device_id=peer, device_id_type=pl.DeviceIdType.MESH
        )

    def remote(src, dst, ss, rs, dev):
        return pltpu.make_async_remote_copy(
            src_ref=src,
            dst_ref=dst,
            send_sem=ss,
            recv_sem=rs,
            device_id=dev,
            device_id_type=pl.DeviceIdType.MESH,
        )

    def side(s):
        return 0 if s == 1 else 1

    def rs_copy(it, s, d):
        i = (it, side(s), d - 1, pl.ds(0, half(s, d)[1]))
        return remote(
            rs_s.at[i], rs_r.at[i], ring_send.at[it, 0, side(s), d - 1],
            ring_recv.at[it, 0, side(s), d - 1], zdev(s * (d - PARENT[d])),
        )

    def ag_part(it, p, s, d):
        start, size = half(s, d)
        return pt.at[it + 1, p, pl.ds(pl.multiple_of(own + start, 32), size), :]

    def ag_copy(it, s, d):
        return remote(
            ag_part(it, POS[-s * PARENT[d]], s, d), ag_part(it, POS[-s * d], s, d),
            ring_send.at[it, 1, side(s), d - 1],
            ring_recv.at[it, 1, side(s), d - 1], zdev(s * (d - PARENT[d])),
        )

    def sib_rs(it, lo, hi):
        return remote(
            ap.at[it, lo:hi, pl.ds(oth, H), :], sib.at[it, lo:hi],
            sib_send.at[it, 0, lo], sib_recv.at[it, 0, lo], sibling,
        )

    def sib_ag(it, n, rows):
        lo, hi = GROUPS[n]
        part = pt.at[it + 1, lo:hi, pl.ds(rows, H), :]
        return remote(part, part, sib_send.at[it, 1, lo], sib_recv.at[it, 1, lo], sibling)

    def f_rs1(it, h, d):
        if h == 0:
            dest, dev = (x + d) % NX, xdev(d)
        else:
            dest, dev = (y + d) % NY, ydev(d)
        return remote(
            fp.at[it, pl.ds(2 * dest, 2), pl.ds(h * H, H), :], rx.at[it, h, d - 1],
            f_send.at[it, h, 0, d - 1], f_recv.at[it, h, 0, d - 1], dev,
        )

    def f_rs2(it, h, d):
        if h == 0:
            dest, dev = (y + d) % NY, ydev(d)
        else:
            dest, dev = (x + d) % NX, xdev(d)
        b, s0 = sub(h, dest)
        return remote(
            g.at[it, h, b, pl.ds(s0, FR), :], ry.at[it, h, d - 1],
            f_send.at[it, h, 1, d - 1], f_recv.at[it, h, 1, d - 1], dev,
        )

    def f_ag1(it, h, d, k):
        b, s0 = sub(h, k)
        part = dt.at[it + 1, 2 * outer[h] + b, pl.ds(h * H + s0, FR), :]
        return remote(
            part, part, f_send.at[it, h, 2, d - 1], f_recv.at[it, h, 2, d - 1],
            ydev(d) if h == 0 else xdev(d),
        )

    def f_ag2(it, h, d, k):
        part = dt.at[it + 1, pl.ds(2 * k, 2), pl.ds(h * H, H), :]
        return remote(
            part, part, f_send.at[it, h, 3, d - 1], f_recv.at[it, h, 3, d - 1],
            xdev(d) if h == 0 else ydev(d),
        )

    far_first = (2, 1, 3)

    def build(lo, hi):
        def rows_of(r, _):
            r0 = pl.multiple_of(r * T, T)
            for p in range(lo, hi):
                idx = inv_ref[r * CB + block_at(p)]
                tile = tiles[jnp.maximum(idx, 0)].astype(jnp.float32)
                tile = jnp.where(idx >= 0, tile, 0.0).astype(jnp.bfloat16)
                kd[pl.ds(r0, T), p * T : (p + 1) * T] = tile
            return 0

        lax.fori_loop(0, RB, rows_of, 0)

    def iteration(it, _):
        def adjoint(lo, hi):
            @pl.when(it == 0)
            def _():
                build(lo, hi)

            for p in range(lo, hi, 2):
                n = min(2, hi - p)
                res = jnp.dot(
                    dl[...],
                    kd[:, p * T : (p + n) * T],
                    preferred_element_type=jnp.float32,
                )
                for k in range(n):
                    ap[it, p + k] = res[:, k * T : (k + 1) * T]
            sib_rs(it, lo, hi).start()

        def rs_node(s, d):
            p = POS[s * d]
            start, size = half(s, d)
            value = (
                ap[it, p, pl.ds(pl.multiple_of(own + start, 32), size), :]
                + sib[it, p, start : start + size, :]
            )
            full = []
            for c in children(d):
                rs_copy(it, s, c).wait_recv()
                if c != 8:
                    value = value + rs_r[it, side(s), c - 1]
                else:
                    full.append(c)
            rs_s[it, side(s), d - 1, :size] = value
            for c in full:
                at, many = half(s, c)
                rows = slice(at, at + many)
                rs_s[it, side(s), d - 1, rows] = (
                    rs_s[it, side(s), d - 1, rows] + rs_r[it, side(s), c - 1, :many]
                )
            rs_copy(it, s, d).start()

        @pl.when(it == 0)
        def _():
            loads[0].wait()
            for b in range(RB):
                dt[0, b] = dual0[b].T
            loads[1].wait()

        for b in range(RB):
            dl[:, b * T : (b + 1) * T] = dt[it, b].astype(jnp.bfloat16)

        @pl.when(it == 0)
        def _():
            pl.semaphore_wait(barrier, len(peers))

        adjoint(11, 16)
        adjoint(5, 11)
        sib_rs(it, 11, 16).wait_recv()
        for d in LEVELS[3]:
            for s in (1, -1):
                rs_node(s, d)
        adjoint(0, 5)
        sib_rs(it, 5, 11).wait_recv()
        for d in LEVELS[2]:
            for s in (1, -1):
                rs_node(s, d)

        @pl.when(it == 0)
        def _():
            for load in loads[2:]:
                load.wait()
            for p in range(CB):
                pt[0, p] = primal0[block_at(p)].T
            for h in range(2):
                dem[h] = dem0[h].T

        sib_rs(it, 0, 5).wait_recv()
        for d in LEVELS[1]:
            for s in (1, -1):
                rs_node(s, d)

        total = ap[it, 0, pl.ds(own, H), :] + sib[it, 0]
        for d in reversed(LEVELS[1]):
            for s in (1, -1):
                rs_copy(it, s, d).wait_recv()
                total = total + rs_r[it, side(s), d - 1]
        old = pt[it, 0, pl.ds(own, H), :]
        pt[it + 1, 0, pl.ds(own, H), :] = jnp.minimum(
            jnp.maximum(old - primal_step * (cost[pl.ds(z, 1), :] - total), 0.0),
            cap[pl.ds(z, 1), :],
        )
        for d in LEVELS[1]:
            for s in (1, -1):
                ag_copy(it, s, d).start()
        sib_ag(it, 0, own).start()

        def ag_level(n, order):
            for d in order:
                for s in (1, -1):
                    ag_copy(it, s, d).wait_recv()
                    for c in reversed(children(d)):
                        ag_copy(it, s, c).start()
            sib_ag(it, n, own).start()

        def forward(lo, hi, first):
            for p in range(lo, hi):
                ext[:, p * T : (p + 1) * T] = (
                    2.0 * pt[it + 1, p] - pt[it, p]
                ).astype(jnp.bfloat16)
            for n in range(0, RB, 2):
                res = lax.dot_general(
                    ext[:, lo * T : hi * T],
                    kd[n * T : (n + 2) * T, lo * T : hi * T],
                    (((1,), (1,)), ((), ())),
                    preferred_element_type=jnp.float32,
                )
                for k in range(2):
                    part = res[:, k * T : (k + 1) * T]
                    fp[it, n + k] = part if first else fp[it, n + k] + part

        ag_level(1, (1, 4))
        ag_level(2, (2, 5, 7))
        sib_ag(it, 0, oth).wait_recv()
        sib_ag(it, 1, oth).wait_recv()
        forward(0, 5, True)
        ag_level(3, (3, 6, 8))
        sib_ag(it, 2, oth).wait_recv()
        forward(5, 11, False)
        sib_ag(it, 3, oth).wait_recv()
        forward(11, 16, False)

        for d in far_first:
            f_rs1(it, 0, d).start()
            f_rs1(it, 1, d).start()

        @pl.when(it == ITERS - 1)
        def _():
            for p in range(CB):
                primal_out[block_at(p)] = pt[ITERS, p].T

        for h in range(2):
            for d in (1, 2, 3):
                f_rs1(it, h, d).wait_recv()
            rows = pl.ds(h * H, H)
            for b in range(2):
                g[it, h, b] = (
                    fp[it, 2 * outer[h] + b, rows, :]
                    + rx[it, h, 0, b]
                    + rx[it, h, 1, b]
                    + rx[it, h, 2, b]
                )
            for d in far_first:
                f_rs2(it, h, d).start()
        for h in range(2):
            for d in (1, 2, 3):
                f_rs2(it, h, d).wait_recv()
            b, s0 = sub(h, inner[h])
            forward = (
                g[it, h, b, pl.ds(s0, FR), :]
                + ry[it, h, 0]
                + ry[it, h, 1]
                + ry[it, h, 2]
            )
            block = 2 * outer[h] + b
            rows = pl.multiple_of(h * H + s0, FR)
            new = dt[it, block, pl.ds(rows, FR), :] + dual_step * (
                dem[h, pl.ds(rows, FR), :] - forward
            )
            new = jnp.where(
                kind[pl.ds(block, 1), :] == 1, jnp.maximum(new, 0.0), new
            )
            dt[it + 1, block, pl.ds(rows, FR), :] = new
            for d in far_first:
                f_ag1(it, h, d, inner[h]).start()
        for h in range(2):
            for d in (1, 2, 3):
                f_ag1(it, h, d, (inner[h] - d + 4) % 4).wait_recv()
            for d in far_first:
                f_ag2(it, h, d, outer[h]).start()
        for h in range(2):
            for d in (1, 2, 3):
                f_ag2(it, h, d, (outer[h] - d + 4) % 4).wait_recv()
        return 0

    lax.fori_loop(0, ITERS, iteration, 0)
    for b in range(RB):
        dual_out[b] = dt[ITERS, b].T

    def drain(it, _):
        for s in (1, -1):
            for d in PARENT:
                rs_copy(it, s, d).wait_send()
                ag_copy(it, s, d).wait_send()
        for n in range(4):
            sib_ag(it, n, own).wait_send()
        for lo, hi in ((0, 5), (5, 11), (11, 16)):
            sib_rs(it, lo, hi).wait_send()
        for h in range(2):
            for d in (1, 2, 3):
                f_rs1(it, h, d).wait_send()
                f_rs2(it, h, d).wait_send()
                f_ag1(it, h, d, inner[h]).wait_send()
                f_ag2(it, h, d, outer[h]).wait_send()
        return 0

    lax.fori_loop(0, ITERS, drain, 0)


def per_device(
    tile_values,
    tile_row,
    tile_column,
    unit_cost,
    capacity,
    demand,
    row_kind,
    primal_start,
    dual_start,
):
    place = jnp.where(tile_row < RB, tile_row * CB + tile_column, RB * CB)
    slot = jnp.arange(SLOTS, dtype=jnp.int32)
    hit = place[:, None] == jnp.arange(RB * CB, dtype=jnp.int32)[None, :]
    inv = jnp.max(jnp.where(hit, slot[:, None], -1), axis=0)
    vmem = pl.BlockSpec(memory_space=pltpu.VMEM)
    f32, bf16 = jnp.float32, jnp.bfloat16
    dma = pltpu.SemaphoreType.DMA
    return pl.pallas_call(
        kernel,
        out_shape=(
            jax.ShapeDtypeStruct((CB, T, S), f32),
            jax.ShapeDtypeStruct((RB, T, S), f32),
        ),
        in_specs=[pl.BlockSpec(memory_space=pltpu.SMEM)]
        + [pl.BlockSpec(memory_space=pl.ANY)] * 7,
        out_specs=(vmem, vmem),
        scratch_shapes=[
            pltpu.VMEM((SLOTS, T, T), bf16),
            pltpu.VMEM((CB, T), f32),
            pltpu.VMEM((CB, T), f32),
            pltpu.VMEM((RB, T), jnp.int32),
            pltpu.VMEM((CB, T, S), f32),
            pltpu.VMEM((RB, T, S), f32),
            pltpu.VMEM((2, T, S), f32),
            pltpu.VMEM((RB * T, CB * T), bf16),
            pltpu.VMEM((ITERS + 1, CB, S, T), f32),
            pltpu.VMEM((ITERS + 1, RB, S, T), f32),
            pltpu.VMEM((S, RB * T), bf16),
            pltpu.VMEM((S, CB * T), bf16),
            pltpu.VMEM((ITERS, CB, S, T), f32),
            pltpu.VMEM((ITERS, CB, H, T), f32),
            pltpu.VMEM((ITERS, 2, 8, H, T), f32),
            pltpu.VMEM((ITERS, 2, 8, H, T), f32),
            pltpu.VMEM((ITERS, RB, S, T), f32),
            pltpu.VMEM((ITERS, 2, 3, 2, H, T), f32),
            pltpu.VMEM((ITERS, 2, 2, H, T), f32),
            pltpu.VMEM((ITERS, 2, 3, FR, T), f32),
            pltpu.VMEM((2, S, T), f32),
            dma((8,)),
            dma((ITERS, 2, 2, 8)),
            dma((ITERS, 2, 2, 8)),
            dma((ITERS, 2, CB)),
            dma((ITERS, 2, CB)),
            dma((ITERS, 2, 4, 3)),
            dma((ITERS, 2, 4, 3)),
        ],
        compiler_params=pltpu.CompilerParams(
            collective_id=0, has_side_effects=True, vmem_limit_bytes=56 << 20
        ),
        cost_estimate=pl.CostEstimate(
            flops=8 * SLOTS * T * T * S, bytes_accessed=6 << 20, transcendentals=0
        ),
    )(
        inv,
        tile_values,
        unit_cost,
        capacity,
        demand,
        row_kind,
        primal_start,
        dual_start,
    )


def solution(mesh):
    placed = (
        P(("col", "row"), None, None),
        P(("col", "row")),
        P(("col", "row")),
        P("col", None),
        P("col", None),
        P("row", None, None),
        P("row", None),
        P("col", None, None),
        P("row", None, None),
    )
    return jax.shard_map(
        per_device,
        mesh=mesh,
        in_specs=placed,
        out_specs=(P("col", None, None), P("row", None, None)),
        check_vma=False,
    )
```

time: 161 us -> 123 us (0.76)
  Pallas kernels: 150 us -> 117 us
  local copies, waits for them, and re-layouts: 8.55 us -> 3.15 us
    pallas_call x1, Pallas kernels: 150 us -> 117 us  [per_device(): pl.pallas_call(kernel, out_shape=(jax.ShapeDtypeStruct((CB, T, S), f32),...]
    unnamed x16 -> x4, local copies, waits for them, and re-layouts: 8.55 us -> 3.15 us
where the time goes in v2:
time: 123 us; the launch traced here: 122 us
  Pallas kernels  117 us (95%)
  local copies, waits for them, and re-layouts  3.15 us (3%)
  other arithmetic  1.28 us (1%)
    pallas_call x1, Pallas kernels, per_device(): pl.pallas_call(kernel, out_shape=(jax.ShapeDtypeStruct((CB, T, S), f32),...  117 us
    unnamed x4, local copies, waits for them, and re-layouts  3.15 us

profile of v2, /device:TPU:1, one launch (start us, length us, event | category | flops | bytes accessed | tf_op | source)
XLA Modules:
  0.0 122.1 jit_solution(14009182979519861010)
XLA Ops:
  0.6 0.7 compare_select_fusion
  1.3 0.6 select_reduce_fusion.inv_ref
  1.9 117.0 %shard_map.104 = (f32[16,128,128]{2,1,0:T(8,128)}, f32[8,128,128]{2,1,0:T(8,128)}) custom-call(s32[128]{0:T(128)} %select_reduce_fusion.inv_ref, bf16[48,128,128]{2,1,0:T(8,128)(2,1)} %tiles_hbm.1, f32[16,128]{1,0:T(8,128)} %cost_hbm.1, f32[16,128]{1,0:T(8,128)} %cap_hbm.1, f32[8,128,128]{2,1,0:T(8,128)} %demand_hbm.1, s32[8,128]{1,0:T(8,128)} %kind_hbm.1, ...), custom_call_target="tpu_custom_call" | custom-call | flops 805306368 | bytes 6291456 | tf_op jit(solution)/shard_map/pallas_call | solution.py:447
  118.9 0.0 copy-start
  118.9 2.4 %copy.13 = f32[16,128,128]{2,1,0:T(8,128)} copy(f32[16,128,128]{2,1,0:T(8,128)} %get-tuple-element.4) | data formatting | bytes 2097152
  121.3 0.0 copy-done
  121.3 0.8 copy.14
Async XLA Ops:
  118.9 2.4 %copy-start = (f32[8,128,128]{2,1,0:T(8,128)S(1)}, f32[8,128,128]{2,1,0:T(8,128)}, u32[]{:S(2)}) copy-start(f32[8,128,128]{2,1,0:T(8,128)} %get-tuple-element.5) | copy-start | bytes 1572868

commit v3 on v2

v3 whole, which is shorter than its diff:
```python
import jax
import jax.numpy as jnp
from jax import lax
from jax.experimental import pallas as pl
from jax.experimental.pallas import tpu as pltpu
from jax.sharding import PartitionSpec as P

ITERS = 2
NX, NY, NZ = 4, 4, 16
RB, CB, T, S = 8, 16, 128, 128
NQ = 2
SQ = S // NQ
H = SQ // 2
FR = H // 2
SLOTS = 48

PARENT = {1: 0, 4: 0, 2: 1, 5: 4, 7: 4, 3: 2, 6: 5, 8: 7}
LEVELS = ((0,), (4, 1), (7, 5, 2), (8, 6, 3))
OFFS = (0, 1, -1, 4, -4, 2, -2, 5, -5, 7, -7, 3, -3, 6, -6, 8)
POS = {o: p for p, o in enumerate(OFFS)}
POS[-8] = POS[8]
PARTS = ((0, 5), (5, 11), (11, 16))
GROUPS = ((0, 1), (1, 5), (5, 11), (11, 16))
HOPS = sorted({s * (d - u) for d, u in PARENT.items() for s in (1, -1)})

primal_step = 0.5
dual_step = 0.5


def children(d):
    return [c for c, u in PARENT.items() if u == d]


def half(s, d):
    if d == 8:
        return (0 if s == 1 else H // 2), H // 2
    return 0, H


def kernel(
    inv_ref,
    tiles_hbm,
    cost_hbm,
    cap_hbm,
    demand_hbm,
    kind_hbm,
    primal_hbm,
    dual_hbm,
    primal_out,
    dual_out,
    tiles,
    cost,
    cap,
    kind,
    primal0,
    dual0,
    dem0,
    kd,
    pt,
    dt,
    dl,
    ext,
    ap,
    sib,
    rs_s,
    rs_r,
    fp,
    rx,
    g,
    ry,
    dem,
    local_sem,
    ring_send,
    ring_recv,
    sib_send,
    sib_recv,
    f_send,
    f_recv,
):
    col = lax.axis_index("col")
    row = lax.axis_index("row")
    x, y = col // NY, col % NY
    z, core = row // 2, row % 2

    def own(q):
        return pl.multiple_of(q * SQ + core * H, H)

    def oth(q):
        return pl.multiple_of(q * SQ + (1 - core) * H, H)

    outer = (x, y)
    inner = (y, x)

    def block_at(p):
        return (z + OFFS[p] + NZ) % NZ

    def zdev(d):
        return (col, ((z + d + NZ) % NZ) * 2 + core)

    sibling = (col, z * 2 + 1 - core)

    def xdev(d):
        return (((x + d) % NX) * NY + y, row)

    def ydev(d):
        return (x * NY + (y + d) % NY, row)

    def sub(k):
        return k // 2, pl.multiple_of((k % 2) * FR, FR)

    dem_block = [2 * outer[h] + sub(inner[h])[0] for h in range(2)]
    loads = [
        pltpu.make_async_copy(src, dst, local_sem.at[n])
        for n, (src, dst) in enumerate(
            [
                (dual_hbm, dual0),
                (tiles_hbm, tiles),
                (primal_hbm, primal0),
                (cost_hbm, cost),
                (cap_hbm, cap),
                (kind_hbm, kind),
                (demand_hbm.at[dem_block[0]], dem0.at[0]),
                (demand_hbm.at[dem_block[1]], dem0.at[1]),
            ]
        )
    ]
    for load in loads:
        load.start()

    barrier = pltpu.get_barrier_semaphore()
    peers = [zdev(d) for d in HOPS] + [sibling]
    peers += [xdev(d) for d in (1, 2, 3)] + [ydev(d) for d in (1, 2, 3)]
    for peer in peers:
        pl.semaphore_signal(
            barrier, inc=1, device_id=peer, device_id_type=pl.DeviceIdType.MESH
        )

    def remote(src, dst, ss, rs, dev):
        return pltpu.make_async_remote_copy(
            src_ref=src,
            dst_ref=dst,
            send_sem=ss,
            recv_sem=rs,
            device_id=dev,
            device_id_type=pl.DeviceIdType.MESH,
        )

    def side(s):
        return 0 if s == 1 else 1

    def rs_copy(it, q, s, d):
        i = (it, q, side(s), d - 1, pl.ds(0, half(s, d)[1]))
        return remote(
            rs_s.at[i], rs_r.at[i], ring_send.at[it, 0, q, side(s), d - 1],
            ring_recv.at[it, 0, q, side(s), d - 1], zdev(s * (d - PARENT[d])),
        )

    def own_rows(q, s, d):
        start, size = half(s, d)
        return pl.ds(pl.multiple_of(own(q) + start, 16), size)

    def ag_copy(it, q, s, d):
        rows = own_rows(q, s, d)
        return remote(
            pt.at[it + 1, POS[-s * PARENT[d]], rows, :],
            pt.at[it + 1, POS[-s * d], rows, :],
            ring_send.at[it, 1, q, side(s), d - 1],
            ring_recv.at[it, 1, q, side(s), d - 1], zdev(s * (d - PARENT[d])),
        )

    def sib_rs(it, q, n):
        lo, hi = PARTS[n]
        return remote(
            ap.at[it, lo:hi, pl.ds(oth(q), H), :], sib.at[it, q, lo:hi],
            sib_send.at[it, 0, q, n], sib_recv.at[it, 0, q, n], sibling,
        )

    def sib_ag(it, q, n, rows):
        lo, hi = GROUPS[n]
        part = pt.at[it + 1, lo:hi, pl.ds(rows, H), :]
        return remote(
            part, part, sib_send.at[it, 1, q, n], sib_recv.at[it, 1, q, n], sibling
        )

    def f_dev(h, d, first):
        return xdev(d) if (h == 0) == first else ydev(d)

    def f_sem(it, q, h, phase, d):
        i = (it, q, h, phase, d - 1)
        return f_send.at[i], f_recv.at[i]

    def f_rs1(it, q, h, d):
        dest = (outer[h] + d) % 4
        return remote(
            fp.at[it, pl.ds(2 * dest, 2), pl.ds(q * SQ + h * H, H), :],
            rx.at[it, q, h, d - 1], *f_sem(it, q, h, 0, d), f_dev(h, d, True),
        )

    def f_rs2(it, q, h, d):
        b, s0 = sub((inner[h] + d) % 4)
        return remote(
            g.at[it, q, h, b, pl.ds(s0, FR), :], ry.at[it, q, h, d - 1],
            *f_sem(it, q, h, 1, d), f_dev(h, d, False),
        )

    def f_rows(q, h, s0):
        return pl.ds(pl.multiple_of(q * SQ + h * H + s0, FR), FR)

    def f_ag1(it, q, h, d, k):
        b, s0 = sub(k)
        part = dt.at[it + 1, 2 * outer[h] + b, f_rows(q, h, s0), :]
        return remote(part, part, *f_sem(it, q, h, 2, d), f_dev(h, d, False))

    def f_ag2(it, q, h, d, k):
        part = dt.at[it + 1, pl.ds(2 * k, 2), pl.ds(q * SQ + h * H, H), :]
        return remote(part, part, *f_sem(it, q, h, 3, d), f_dev(h, d, True))

    far_first = (2, 1, 3)

    def build(lo, hi):
        def rows_of(r, _):
            r0 = pl.multiple_of(r * T, T)
            for p in range(lo, hi):
                idx = inv_ref[r * CB + block_at(p)]
                tile = tiles[jnp.maximum(idx, 0)]
                tile = jnp.where(idx >= 0, tile, jnp.zeros_like(tile))
                kd[pl.ds(r0, T), p * T : (p + 1) * T] = tile
            return 0

        lax.fori_loop(0, RB, rows_of, 0)

    def f_ag2_wait(it, q):
        for h in range(2):
            for d in (1, 2, 3):
                f_ag2(it, q, h, d, (outer[h] - d + 4) % 4).wait_recv()

    both = (0, S)

    def slab(q):
        return (q * SQ, SQ)

    def iteration(it, _):
        def adjoint(n, rows):
            lo, hi = PARTS[n]
            r0, many = rows
            for p in range(lo, hi, 2):
                w = min(2, hi - p)
                res = jnp.dot(
                    dl[r0 : r0 + many, :],
                    kd[:, p * T : (p + w) * T],
                    preferred_element_type=jnp.float32,
                )
                for k in range(w):
                    ap[it, p + k, r0 : r0 + many] = res[:, k * T : (k + 1) * T]

        def build_first(n):
            @pl.when(it == 0)
            def _():
                build(*PARTS[n])

        def rs_node(q, s, d):
            p = POS[s * d]
            start, size = half(s, d)
            value = (
                ap[it, p, own_rows(q, s, d), :] + sib[it, q, p, start : start + size, :]
            )
            for c in children(d):
                rs_copy(it, q, s, c).wait_recv()
                if c != 8:
                    value = value + rs_r[it, q, side(s), c - 1]
            rs_s[it, q, side(s), d - 1, :size] = value
            if 8 in children(d):
                at, many = half(s, 8)
                rows = slice(at, at + many)
                rs_s[it, q, side(s), d - 1, rows] = (
                    rs_s[it, q, side(s), d - 1, rows] + rs_r[it, q, side(s), 7, :many]
                )
            rs_copy(it, q, s, d).start()

        def rs_level(n):
            for q in range(NQ):
                sib_rs(it, q, n - 1).wait_recv()
                for d in LEVELS[n]:
                    for s in (1, -1):
                        rs_node(q, s, d)

        @pl.when(it == 0)
        def _():
            loads[0].wait()
            for b in range(RB):
                dt[0, b] = dual0[b].T
            loads[1].wait()
            build(*PARTS[2])
            pl.semaphore_wait(barrier, len(peers))

        for q in range(NQ):

            @pl.when(it > 0)
            def _():
                f_ag2_wait(it - 1, q)

            r0, many = slab(q)
            for b in range(RB):
                dl[r0 : r0 + many, b * T : (b + 1) * T] = dt[
                    it, b, r0 : r0 + many
                ].astype(jnp.bfloat16)
            adjoint(2, slab(q))
            sib_rs(it, q, 2).start()

        build_first(1)
        adjoint(1, both)
        for q in range(NQ):
            sib_rs(it, q, 1).start()
        rs_level(3)
        build_first(0)
        adjoint(0, both)
        for q in range(NQ):
            sib_rs(it, q, 0).start()
        rs_level(2)

        @pl.when(it == 0)
        def _():
            for load in loads[2:]:
                load.wait()
            for p in range(CB):
                pt[0, p] = primal0[block_at(p)].T
            for h in range(2):
                dem[h] = dem0[h].T

        rs_level(1)

        for q in range(NQ):
            rows = pl.ds(own(q), H)
            total = ap[it, 0, rows, :] + sib[it, q, 0]
            for d in reversed(LEVELS[1]):
                for s in (1, -1):
                    rs_copy(it, q, s, d).wait_recv()
                    total = total + rs_r[it, q, side(s), d - 1]
            old = pt[it, 0, rows, :]
            pt[it + 1, 0, rows, :] = jnp.minimum(
                jnp.maximum(old - primal_step * (cost[pl.ds(z, 1), :] - total), 0.0),
                cap[pl.ds(z, 1), :],
            )
            for d in LEVELS[1]:
                for s in (1, -1):
                    ag_copy(it, q, s, d).start()
            sib_ag(it, q, 0, own(q)).start()

        def ag_level(n):
            for q in range(NQ):
                for d in reversed(LEVELS[n]):
                    for s in (1, -1):
                        ag_copy(it, q, s, d).wait_recv()
                        for c in reversed(children(d)):
                            ag_copy(it, q, s, c).start()
                sib_ag(it, q, n, own(q)).start()

        def forward(lo, hi, rows, first):
            r0, many = rows
            at = slice(r0, r0 + many)
            for p in range(lo, hi):
                ext[at, p * T : (p + 1) * T] = (
                    2.0 * pt[it + 1, p, at] - pt[it, p, at]
                ).astype(jnp.bfloat16)
            for n in range(0, RB, 2):
                res = lax.dot_general(
                    ext[at, lo * T : hi * T],
                    kd[n * T : (n + 2) * T, lo * T : hi * T],
                    (((1,), (1,)), ((), ())),
                    preferred_element_type=jnp.float32,
                )
                for k in range(2):
                    part = res[:, k * T : (k + 1) * T]
                    fp[it, n + k, at] = part if first else fp[it, n + k, at] + part

        ag_level(1)
        ag_level(2)
        for q in range(NQ):
            sib_ag(it, q, 0, oth(q)).wait_recv()
            sib_ag(it, q, 1, oth(q)).wait_recv()
        forward(0, 5, both, True)
        ag_level(3)
        for q in range(NQ):
            sib_ag(it, q, 2, oth(q)).wait_recv()
        forward(5, 11, both, False)

        for q in range(NQ):
            sib_ag(it, q, 3, oth(q)).wait_recv()
            forward(11, 16, slab(q), False)
            for d in far_first:
                for h in range(2):
                    f_rs1(it, q, h, d).start()

        @pl.when(it == ITERS - 1)
        def _():
            for p in range(CB):
                primal_out[block_at(p)] = pt[ITERS, p].T

        for q in range(NQ):
            for h in range(2):
                for d in (1, 3, 2):
                    f_rs1(it, q, h, d).wait_recv()
                for b in range(2):
                    g[it, q, h, b] = (
                        fp[it, 2 * outer[h] + b, q * SQ + h * H : q * SQ + (h + 1) * H]
                        + rx[it, q, h, 0, b]
                        + rx[it, q, h, 1, b]
                        + rx[it, q, h, 2, b]
                    )
                for d in far_first:
                    f_rs2(it, q, h, d).start()
        for q in range(NQ):
            for h in range(2):
                for d in (1, 3, 2):
                    f_rs2(it, q, h, d).wait_recv()
                b, s0 = sub(inner[h])
                forward_sum = (
                    g[it, q, h, b, pl.ds(s0, FR), :]
                    + ry[it, q, h, 0]
                    + ry[it, q, h, 1]
                    + ry[it, q, h, 2]
                )
                block = 2 * outer[h] + b
                rows = f_rows(q, h, s0)
                new = dt[it, block, rows, :] + dual_step * (
                    dem[h, rows, :] - forward_sum
                )
                new = jnp.where(
                    kind[pl.ds(block, 1), :] == 1, jnp.maximum(new, 0.0), new
                )
                dt[it + 1, block, rows, :] = new
                for d in far_first:
                    f_ag1(it, q, h, d, inner[h]).start()
        for q in range(NQ):
            for h in range(2):
                for d in (1, 3, 2):
                    f_ag1(it, q, h, d, (inner[h] - d + 4) % 4).wait_recv()
                for d in far_first:
                    f_ag2(it, q, h, d, outer[h]).start()
        return 0

    lax.fori_loop(0, ITERS, iteration, 0)
    for q in range(NQ):
        f_ag2_wait(ITERS - 1, q)
    for b in range(RB):
        dual_out[b] = dt[ITERS, b].T

    def drain(it, _):
        for q in range(NQ):
            for s in (1, -1):
                for d in PARENT:
                    rs_copy(it, q, s, d).wait_send()
                    ag_copy(it, q, s, d).wait_send()
            for n in range(len(GROUPS)):
                sib_ag(it, q, n, own(q)).wait_send()
            for n in range(len(PARTS)):
                sib_rs(it, q, n).wait_send()
            for h in range(2):
                for d in (1, 2, 3):
                    f_rs1(it, q, h, d).wait_send()
                    f_rs2(it, q, h, d).wait_send()
                    f_ag1(it, q, h, d, inner[h]).wait_send()
                    f_ag2(it, q, h, d, outer[h]).wait_send()
        return 0

    lax.fori_loop(0, ITERS, drain, 0)


def per_device(
    tile_values,
    tile_row,
    tile_column,
    unit_cost,
    capacity,
    demand,
    row_kind,
    primal_start,
    dual_start,
):
    place = jnp.where(tile_row < RB, tile_row * CB + tile_column, RB * CB)
    slot = jnp.arange(SLOTS, dtype=jnp.int32)
    hit = place[:, None] == jnp.arange(RB * CB, dtype=jnp.int32)[None, :]
    inv = jnp.max(jnp.where(hit, slot[:, None], -1), axis=0)
    vmem = pl.BlockSpec(memory_space=pltpu.VMEM)
    f32, bf16 = jnp.float32, jnp.bfloat16
    dma = pltpu.SemaphoreType.DMA
    return pl.pallas_call(
        kernel,
        out_shape=(
            jax.ShapeDtypeStruct((CB, T, S), f32),
            jax.ShapeDtypeStruct((RB, T, S), f32),
        ),
        in_specs=[pl.BlockSpec(memory_space=pltpu.SMEM)]
        + [pl.BlockSpec(memory_space=pl.ANY)] * 7,
        out_specs=(vmem, vmem),
        scratch_shapes=[
            pltpu.VMEM((SLOTS, T, T), bf16),
            pltpu.VMEM((CB, T), f32),
            pltpu.VMEM((CB, T), f32),
            pltpu.VMEM((RB, T), jnp.int32),
            pltpu.VMEM((CB, T, S), f32),
            pltpu.VMEM((RB, T, S), f32),
            pltpu.VMEM((2, T, S), f32),
            pltpu.VMEM((RB * T, CB * T), bf16),
            pltpu.VMEM((ITERS + 1, CB, S, T), f32),
            pltpu.VMEM((ITERS + 1, RB, S, T), f32),
            pltpu.VMEM((S, RB * T), bf16),
            pltpu.VMEM((S, CB * T), bf16),
            pltpu.VMEM((ITERS, CB, S, T), f32),
            pltpu.VMEM((ITERS, NQ, CB, H, T), f32),
            pltpu.VMEM((ITERS, NQ, 2, 8, H, T), f32),
            pltpu.VMEM((ITERS, NQ, 2, 8, H, T), f32),
            pltpu.VMEM((ITERS, RB, S, T), f32),
            pltpu.VMEM((ITERS, NQ, 2, 3, 2, H, T), f32),
            pltpu.VMEM((ITERS, NQ, 2, 2, H, T), f32),
            pltpu.VMEM((ITERS, NQ, 2, 3, FR, T), f32),
            pltpu.VMEM((2, S, T), f32),
            dma((8,)),
            dma((ITERS, 2, NQ, 2, 8)),
            dma((ITERS, 2, NQ, 2, 8)),
            dma((ITERS, 2, NQ, 4)),
            dma((ITERS, 2, NQ, 4)),
            dma((ITERS, NQ, 2, 4, 3)),
            dma((ITERS, NQ, 2, 4, 3)),
        ],
        compiler_params=pltpu.CompilerParams(
            collective_id=0, has_side_effects=True, vmem_limit_bytes=56 << 20
        ),
        cost_estimate=pl.CostEstimate(
            flops=8 * SLOTS * T * T * S, bytes_accessed=6 << 20, transcendentals=0
        ),
    )(
        inv,
        tile_values,
        unit_cost,
        capacity,
        demand,
        row_kind,
        primal_start,
        dual_start,
    )


def solution(mesh):
    placed = (
        P(("col", "row"), None, None),
        P(("col", "row")),
        P(("col", "row")),
        P("col", None),
        P("col", None),
        P("row", None, None),
        P("row", None),
        P("col", None, None),
        P("row", None, None),
    )
    return jax.shard_map(
        per_device,
        mesh=mesh,
        in_specs=placed,
        out_specs=(P("col", None, None), P("row", None, None)),
        check_vma=False,
    )
```

time: 123 us -> 117 us (0.951)
  Pallas kernels: 117 us -> 110 us
    pallas_call x1, Pallas kernels: 117 us -> 110 us  [per_device(): pl.pallas_call(kernel, out_shape=(jax.ShapeDtypeStruct((CB, T, S), f32),...]
where the time goes in v3:
time: 117 us; the launch traced here: 115 us
  Pallas kernels  110 us (94%)
  local copies, waits for them, and re-layouts  3.15 us (3%)
  other arithmetic  1.28 us (1%)
    pallas_call x1, Pallas kernels, per_device(): pl.pallas_call(kernel, out_shape=(jax.ShapeDtypeStruct((CB, T, S), f32),...  110 us
    unnamed x4, local copies, waits for them, and re-layouts  3.15 us

profile of v3, /device:TPU:1, one launch (start us, length us, event | category | flops | bytes accessed | tf_op | source)
XLA Modules:
  0.0 115.2 jit_solution(8460510909450074518)
XLA Ops:
  0.6 0.7 compare_select_fusion
  1.3 0.6 select_reduce_fusion.inv_ref
  1.9 110.1 %shard_map.104 = (f32[16,128,128]{2,1,0:T(8,128)}, f32[8,128,128]{2,1,0:T(8,128)}) custom-call(s32[128]{0:T(128)} %select_reduce_fusion.inv_ref, bf16[48,128,128]{2,1,0:T(8,128)(2,1)} %tiles_hbm.1, f32[16,128]{1,0:T(8,128)} %cost_hbm.1, f32[16,128]{1,0:T(8,128)} %cap_hbm.1, f32[8,128,128]{2,1,0:T(8,128)} %demand_hbm.1, s32[8,128]{1,0:T(8,128)} %kind_hbm.1, ...), custom_call_target="tpu_custom_call" | custom-call | flops 805306368 | bytes 6291456 | tf_op jit(solution)/shard_map/pallas_call | solution.py:487
  112.0 0.0 copy-start
  112.0 2.4 %copy.13 = f32[16,128,128]{2,1,0:T(8,128)} copy(f32[16,128,128]{2,1,0:T(8,128)} %get-tuple-element.4) | data formatting | bytes 2097152
  114.4 0.0 copy-done
  114.4 0.8 copy.14
Async XLA Ops:
  112.0 2.4 %copy-start = (f32[8,128,128]{2,1,0:T(8,128)S(1)}, f32[8,128,128]{2,1,0:T(8,128)}, u32[]{:S(2)}) copy-start(f32[8,128,128]{2,1,0:T(8,128)} %get-tuple-element.5) | copy-start | bytes 1572868

commit v4 on v3

--- a/solution.py
+++ b/solution.py
@@ -79,36 +79,44 @@
 ):
     col = lax.axis_index("col")
     row = lax.axis_index("row")
-    x, y = col // NY, col % NY
-    z, core = row // 2, row % 2
-
-    def own(q):
-        return pl.multiple_of(q * SQ + core * H, H)
-
-    def oth(q):
-        return pl.multiple_of(q * SQ + (1 - core) * H, H)
-
+    x, y = lax.div(col, NY), lax.rem(col, NY)
+    z, core = lax.div(row, 2), lax.rem(row, 2)
     outer = (x, y)
     inner = (y, x)
+    own_at = [pl.multiple_of(q * SQ + core * H, H) for q in range(NQ)]
+    oth_at = [pl.multiple_of(q * SQ + (1 - core) * H, H) for q in range(NQ)]
+    block_of = [lax.rem(z + OFFS[p] + NZ, NZ) for p in range(CB)]
+    z_row = {d: lax.rem(z + d + NZ, NZ) * 2 + core for d in HOPS}
+    sibling = (col, z * 2 + 1 - core)
+    x_at = [lax.rem(x + d, NX) for d in range(NX)]
+    y_at = [lax.rem(y + d, NY) for d in range(NY)]
+    outer_at, inner_at = (x_at, y_at), (y_at, x_at)
+    x_col = [x_at[d] * NY + y for d in range(NX)]
+    y_col = [x * NY + y_at[d] for d in range(NY)]
+
+    def own(q):
+        return own_at[q]
+
+    def oth(q):
+        return oth_at[q]
 
     def block_at(p):
-        return (z + OFFS[p] + NZ) % NZ
+        return block_of[p]
 
     def zdev(d):
-        return (col, ((z + d + NZ) % NZ) * 2 + core)
-
-    sibling = (col, z * 2 + 1 - core)
+        return (col, z_row[d])
 
     def xdev(d):
-        return (((x + d) % NX) * NY + y, row)
+        return (x_col[d], row)
 
     def ydev(d):
-        return (x * NY + (y + d) % NY, row)
+        return (y_col[d], row)
 
     def sub(k):
-        return k // 2, pl.multiple_of((k % 2) * FR, FR)
-
-    dem_block = [2 * outer[h] + sub(inner[h])[0] for h in range(2)]
+        return lax.div(k, 2), pl.multiple_of(lax.rem(k, 2) * FR, FR)
+
+    sub_at = [[sub(inner_at[h][d]) for d in range(4)] for h in range(2)]
+    dem_block = [2 * outer[h] + sub_at[h][0][0] for h in range(2)]
     loads = [
         pltpu.make_async_copy(src, dst, local_sem.at[n])
         for n, (src, dst) in enumerate(
@@ -190,14 +198,14 @@
         return f_send.at[i], f_recv.at[i]
 
     def f_rs1(it, q, h, d):
-        dest = (outer[h] + d) % 4
+        dest = outer_at[h][d]
         return remote(
             fp.at[it, pl.ds(2 * dest, 2), pl.ds(q * SQ + h * H, H), :],
             rx.at[it, q, h, d - 1], *f_sem(it, q, h, 0, d), f_dev(h, d, True),
         )
 
     def f_rs2(it, q, h, d):
-        b, s0 = sub((inner[h] + d) % 4)
+        b, s0 = sub_at[h][d]
         return remote(
             g.at[it, q, h, b, pl.ds(s0, FR), :], ry.at[it, q, h, d - 1],
             *f_sem(it, q, h, 1, d), f_dev(h, d, False),
@@ -207,12 +215,12 @@
         return pl.ds(pl.multiple_of(q * SQ + h * H + s0, FR), FR)
 
     def f_ag1(it, q, h, d, k):
-        b, s0 = sub(k)
+        b, s0 = sub_at[h][k]
         part = dt.at[it + 1, 2 * outer[h] + b, f_rows(q, h, s0), :]
         return remote(part, part, *f_sem(it, q, h, 2, d), f_dev(h, d, False))
 
     def f_ag2(it, q, h, d, k):
-        part = dt.at[it + 1, pl.ds(2 * k, 2), pl.ds(q * SQ + h * H, H), :]
+        part = dt.at[it + 1, pl.ds(2 * outer_at[h][k], 2), pl.ds(q * SQ + h * H, H), :]
         return remote(part, part, *f_sem(it, q, h, 3, d), f_dev(h, d, True))
 
     far_first = (2, 1, 3)
@@ -232,9 +240,7 @@
     def f_ag2_wait(it, q):
         for h in range(2):
             for d in (1, 2, 3):
-                f_ag2(it, q, h, d, (outer[h] - d + 4) % 4).wait_recv()
-
-    both = (0, S)
+                f_ag2(it, q, h, d, 4 - d).wait_recv()
 
     def slab(q):
         return (q * SQ, SQ)
@@ -277,12 +283,11 @@
                 )
             rs_copy(it, q, s, d).start()
 
-        def rs_level(n):
-            for q in range(NQ):
-                sib_rs(it, q, n - 1).wait_recv()
-                for d in LEVELS[n]:
-                    for s in (1, -1):
-                        rs_node(q, s, d)
+        def rs_level(n, q):
+            sib_rs(it, q, n - 1).wait_recv()
+            for d in LEVELS[n]:
+                for s in (1, -1):
+                    rs_node(q, s, d)
 
         @pl.when(it == 0)
         def _():
@@ -293,8 +298,11 @@
             build(*PARTS[2])
             pl.semaphore_wait(barrier, len(peers))
 
-        for q in range(NQ):
-
+        def partial(q, n):
+            adjoint(n, slab(q))
+            sib_rs(it, q, n).start()
+
+        def begin(q):
             @pl.when(it > 0)
             def _():
                 f_ag2_wait(it - 1, q)
@@ -304,19 +312,20 @@
                 dl[r0 : r0 + many, b * T : (b + 1) * T] = dt[
                     it, b, r0 : r0 + many
                 ].astype(jnp.bfloat16)
-            adjoint(2, slab(q))
-            sib_rs(it, q, 2).start()
-
+            partial(q, 2)
+
+        begin(0)
         build_first(1)
-        adjoint(1, both)
-        for q in range(NQ):
-            sib_rs(it, q, 1).start()
-        rs_level(3)
+        partial(0, 1)
+        begin(1)
+        rs_level(3, 0)
+        partial(1, 1)
+        rs_level(3, 1)
         build_first(0)
-        adjoint(0, both)
-        for q in range(NQ):
-            sib_rs(it, q, 0).start()
-        rs_level(2)
+        partial(0, 0)
+        partial(1, 0)
+        for q in range(NQ):
+            rs_level(2, q)
 
         @pl.when(it == 0)
         def _():
@@ -327,7 +336,8 @@
             for h in range(2):
                 dem[h] = dem0[h].T
 
-        rs_level(1)
+        for q in range(NQ):
+            rs_level(1, q)
 
         for q in range(NQ):
             rows = pl.ds(own(q), H)
@@ -346,14 +356,13 @@
                     ag_copy(it, q, s, d).start()
             sib_ag(it, q, 0, own(q)).start()
 
-        def ag_level(n):
-            for q in range(NQ):
-                for d in reversed(LEVELS[n]):
-                    for s in (1, -1):
-                        ag_copy(it, q, s, d).wait_recv()
-                        for c in reversed(children(d)):
-                            ag_copy(it, q, s, c).start()
-                sib_ag(it, q, n, own(q)).start()
+        def ag_level(n, q):
+            for d in reversed(LEVELS[n]):
+                for s in (1, -1):
+                    ag_copy(it, q, s, d).wait_recv()
+                    for c in reversed(children(d)):
+                        ag_copy(it, q, s, c).start()
+            sib_ag(it, q, n, own(q)).start()
 
         def forward(lo, hi, rows, first):
             r0, many = rows
@@ -373,18 +382,19 @@
                     part = res[:, k * T : (k + 1) * T]
                     fp[it, n + k, at] = part if first else fp[it, n + k, at] + part
 
-        ag_level(1)
-        ag_level(2)
+        for n in (1, 2):
+            for q in range(NQ):
+                ag_level(n, q)
         for q in range(NQ):
             sib_ag(it, q, 0, oth(q)).wait_recv()
             sib_ag(it, q, 1, oth(q)).wait_recv()
-        forward(0, 5, both, True)
-        ag_level(3)
+            forward(0, 5, slab(q), True)
+        for q in range(NQ):
+            ag_level(3, q)
+
         for q in range(NQ):
             sib_ag(it, q, 2, oth(q)).wait_recv()
-        forward(5, 11, both, False)
-
-        for q in range(NQ):
+            forward(5, 11, slab(q), False)
             sib_ag(it, q, 3, oth(q)).wait_recv()
             forward(11, 16, slab(q), False)
             for d in far_first:
@@ -395,6 +405,16 @@
         def _():
             for p in range(CB):
                 primal_out[block_at(p)] = pt[ITERS, p].T
+
+        for q in range(NQ):
+            for s in (1, -1):
+                for d in PARENT:
+                    rs_copy(it, q, s, d).wait_send()
+                    ag_copy(it, q, s, d).wait_send()
+            for n in range(len(GROUPS)):
+                sib_ag(it, q, n, own(q)).wait_send()
+            for n in range(len(PARTS)):
+                sib_rs(it, q, n).wait_send()
 
         for q in range(NQ):
             for h in range(2):
@@ -413,7 +433,7 @@
             for h in range(2):
                 for d in (1, 3, 2):
                     f_rs2(it, q, h, d).wait_recv()
-                b, s0 = sub(inner[h])
+                b, s0 = sub_at[h][0]
                 forward_sum = (
                     g[it, q, h, b, pl.ds(s0, FR), :]
                     + ry[it, q, h, 0]
@@ -430,13 +450,19 @@
                 )
                 dt[it + 1, block, rows, :] = new
                 for d in far_first:
-                    f_ag1(it, q, h, d, inner[h]).start()
+                    f_ag1(it, q, h, d, 0).start()
         for q in range(NQ):
             for h in range(2):
                 for d in (1, 3, 2):
-                    f_ag1(it, q, h, d, (inner[h] - d + 4) % 4).wait_recv()
+                    f_ag1(it, q, h, d, 4 - d).wait_recv()
                 for d in far_first:
-                    f_ag2(it, q, h, d, outer[h]).start()
+                    f_ag2(it, q, h, d, 0).start()
+        for q in range(NQ):
+            for h in range(2):
+                for d in (1, 2, 3):
+                    f_rs1(it, q, h, d).wait_send()
+                    f_rs2(it, q, h, d).wait_send()
+                    f_ag1(it, q, h, d, 0).wait_send()
         return 0
 
     lax.fori_loop(0, ITERS, iteration, 0)
@@ -445,25 +471,11 @@
     for b in range(RB):
         dual_out[b] = dt[ITERS, b].T
 
-    def drain(it, _):
-        for q in range(NQ):
-            for s in (1, -1):
-                for d in PARENT:
-                    rs_copy(it, q, s, d).wait_send()
-                    ag_copy(it, q, s, d).wait_send()
-            for n in range(len(GROUPS)):
-                sib_ag(it, q, n, own(q)).wait_send()
-            for n in range(len(PARTS)):
-                sib_rs(it, q, n).wait_send()
+    for it in range(ITERS):
+        for q in range(NQ):
             for h in range(2):
                 for d in (1, 2, 3):
-                    f_rs1(it, q, h, d).wait_send()
-                    f_rs2(it, q, h, d).wait_send()
-                    f_ag1(it, q, h, d, inner[h]).wait_send()
-                    f_ag2(it, q, h, d, outer[h]).wait_send()
-        return 0
-
-    lax.fori_loop(0, ITERS, drain, 0)
+                    f_ag2(it, q, h, d, 0).wait_send()
 
 
 def per_device(

time: 117 us -> 116 us (level)
  no operation moved by 1% of the time
where the time goes in v4:
time: 116 us; the launch traced here: 115 us
  Pallas kernels  110 us (95%)
  local copies, waits for them, and re-layouts  3.15 us (3%)
  other arithmetic  1.28 us (1%)
    pallas_call x1, Pallas kernels, per_device(): pl.pallas_call(kernel, out_shape=(jax.ShapeDtypeStruct((CB, T, S), f32),...  110 us
    unnamed x4, local copies, waits for them, and re-layouts  3.15 us

profile of v4, /device:TPU:1, one launch (start us, length us, event | category | flops | bytes accessed | tf_op | source)
XLA Modules:
  0.0 114.7 jit_solution(9083181393650220217)
XLA Ops:
  0.6 0.7 compare_select_fusion
  1.3 0.6 select_reduce_fusion.inv_ref
  1.9 109.6 %shard_map.104 = (f32[16,128,128]{2,1,0:T(8,128)}, f32[8,128,128]{2,1,0:T(8,128)}) custom-call(s32[128]{0:T(128)} %select_reduce_fusion.inv_ref, bf16[48,128,128]{2,1,0:T(8,128)(2,1)} %tiles_hbm.1, f32[16,128]{1,0:T(8,128)} %cost_hbm.1, f32[16,128]{1,0:T(8,128)} %cap_hbm.1, f32[8,128,128]{2,1,0:T(8,128)} %demand_hbm.1, s32[8,128]{1,0:T(8,128)} %kind_hbm.1, ...), custom_call_target="tpu_custom_call" | custom-call | flops 805306368 | bytes 6291456 | tf_op jit(solution)/shard_map/pallas_call | solution.py:499
  111.6 0.0 copy-start
  111.6 2.4 %copy.13 = f32[16,128,128]{2,1,0:T(8,128)} copy(f32[16,128,128]{2,1,0:T(8,128)} %get-tuple-element.4) | data formatting | bytes 2097152
  113.9 0.0 copy-done
  113.9 0.8 copy.14
Async XLA Ops:
  111.6 2.4 %copy-start = (f32[8,128,128]{2,1,0:T(8,128)S(1)}, f32[8,128,128]{2,1,0:T(8,128)}, u32[]{:S(2)}) copy-start(f32[8,128,128]{2,1,0:T(8,128)} %get-tuple-element.5) | copy-start | bytes 1572868

commit v5 on v4

--- a/solution.py
+++ b/solution.py
@@ -20,7 +20,9 @@
 POS = {o: p for p, o in enumerate(OFFS)}
 POS[-8] = POS[8]
 PARTS = ((0, 5), (5, 11), (11, 16))
-GROUPS = ((0, 1), (1, 5), (5, 11), (11, 16))
+GROUPS = ((0, 1), (1, 5), (5, 11))
+LEAVES = LEVELS[3]
+LEAF_HOPS = sorted({s * (d - PARENT[d]) for d in LEAVES for s in (1, -1)})
 HOPS = sorted({s * (d - u) for d, u in PARENT.items() for s in (1, -1)})
 
 primal_step = 0.5
@@ -64,6 +66,7 @@
     sib,
     rs_s,
     rs_r,
+    rs_x,
     fp,
     rx,
     g,
@@ -87,6 +90,7 @@
     oth_at = [pl.multiple_of(q * SQ + (1 - core) * H, H) for q in range(NQ)]
     block_of = [lax.rem(z + OFFS[p] + NZ, NZ) for p in range(CB)]
     z_row = {d: lax.rem(z + d + NZ, NZ) * 2 + core for d in HOPS}
+    cross_row = {d: lax.rem(z + d + NZ, NZ) * 2 + 1 - core for d in LEAF_HOPS}
     sibling = (col, z * 2 + 1 - core)
     x_at = [lax.rem(x + d, NX) for d in range(NX)]
     y_at = [lax.rem(y + d, NY) for d in range(NY)]
@@ -137,6 +141,7 @@
 
     barrier = pltpu.get_barrier_semaphore()
     peers = [zdev(d) for d in HOPS] + [sibling]
+    peers += [(col, cross_row[d]) for d in LEAF_HOPS]
     peers += [xdev(d) for d in (1, 2, 3)] + [ydev(d) for d in (1, 2, 3)]
     for peer in peers:
         pl.semaphore_signal(
@@ -163,17 +168,35 @@
             ring_recv.at[it, 0, q, side(s), d - 1], zdev(s * (d - PARENT[d])),
         )
 
+    def rows_at(first, s, d):
+        start, size = half(s, d)
+        return pl.ds(pl.multiple_of(first + start, 16), size)
+
     def own_rows(q, s, d):
-        start, size = half(s, d)
-        return pl.ds(pl.multiple_of(own(q) + start, 16), size)
-
-    def ag_copy(it, q, s, d):
-        rows = own_rows(q, s, d)
+        return rows_at(own(q), s, d)
+
+    def rs_leaf(it, q, s, d, cross):
+        hop = s * (d - PARENT[d])
+        phase, into = (2, rs_x) if cross else (0, rs_r)
+        rows = rows_at(oth(q) if cross else own(q), s, d)
+        return remote(
+            ap.at[it, POS[s * d], rows, :],
+            into.at[it, q, side(s), d - 1, pl.ds(0, half(s, d)[1])],
+            ring_send.at[it, phase, q, side(s), d - 1],
+            ring_recv.at[it, phase, q, side(s), d - 1],
+            (col, cross_row[hop] if cross else z_row[hop]),
+        )
+
+    def ag_copy(it, q, s, d, cross=False, arrival=False):
+        hop = s * (d - PARENT[d])
+        phase = 3 if cross else 1
+        rows = rows_at(oth(q) if cross and arrival else own(q), s, d)
         return remote(
             pt.at[it + 1, POS[-s * PARENT[d]], rows, :],
             pt.at[it + 1, POS[-s * d], rows, :],
-            ring_send.at[it, 1, q, side(s), d - 1],
-            ring_recv.at[it, 1, q, side(s), d - 1], zdev(s * (d - PARENT[d])),
+            ring_send.at[it, phase, q, side(s), d - 1],
+            ring_recv.at[it, phase, q, side(s), d - 1],
+            (col, cross_row[hop] if cross else z_row[hop]),
         )
 
     def sib_rs(it, q, n):
@@ -271,15 +294,23 @@
                 ap[it, p, own_rows(q, s, d), :] + sib[it, q, p, start : start + size, :]
             )
             for c in children(d):
-                rs_copy(it, q, s, c).wait_recv()
+                if c in LEAVES:
+                    rs_leaf(it, q, s, c, False).wait_recv()
+                    rs_leaf(it, q, s, c, True).wait_recv()
+                else:
+                    rs_copy(it, q, s, c).wait_recv()
                 if c != 8:
                     value = value + rs_r[it, q, side(s), c - 1]
+                if c in (3, 6):
+                    value = value + rs_x[it, q, side(s), c - 1]
             rs_s[it, q, side(s), d - 1, :size] = value
             if 8 in children(d):
                 at, many = half(s, 8)
                 rows = slice(at, at + many)
                 rs_s[it, q, side(s), d - 1, rows] = (
-                    rs_s[it, q, side(s), d - 1, rows] + rs_r[it, q, side(s), 7, :many]
+                    rs_s[it, q, side(s), d - 1, rows]
+                    + rs_r[it, q, side(s), 7, :many]
+                    + rs_x[it, q, side(s), 7, :many]
                 )
             rs_copy(it, q, s, d).start()
 
@@ -312,15 +343,17 @@
                 dl[r0 : r0 + many, b * T : (b + 1) * T] = dt[
                     it, b, r0 : r0 + many
                 ].astype(jnp.bfloat16)
-            partial(q, 2)
+            adjoint(2, slab(q))
+            for d in LEAVES:
+                for s in (1, -1):
+                    rs_leaf(it, q, s, d, False).start()
+                    rs_leaf(it, q, s, d, True).start()
 
         begin(0)
         build_first(1)
         partial(0, 1)
         begin(1)
-        rs_level(3, 0)
         partial(1, 1)
-        rs_level(3, 1)
         build_first(0)
         partial(0, 0)
         partial(1, 0)
@@ -362,6 +395,8 @@
                     ag_copy(it, q, s, d).wait_recv()
                     for c in reversed(children(d)):
                         ag_copy(it, q, s, c).start()
+                        if c in LEAVES:
+                            ag_copy(it, q, s, c, True).start()
             sib_ag(it, q, n, own(q)).start()
 
         def forward(lo, hi, rows, first):
@@ -390,12 +425,12 @@
             sib_ag(it, q, 1, oth(q)).wait_recv()
             forward(0, 5, slab(q), True)
         for q in range(NQ):
-            ag_level(3, q)
-
-        for q in range(NQ):
             sib_ag(it, q, 2, oth(q)).wait_recv()
             forward(5, 11, slab(q), False)
-            sib_ag(it, q, 3, oth(q)).wait_recv()
+            for d in LEAVES:
+                for s in (1, -1):
+                    ag_copy(it, q, s, d).wait_recv()
+                    ag_copy(it, q, s, d, True, True).wait_recv()
             forward(11, 16, slab(q), False)
             for d in far_first:
                 for h in range(2):
@@ -409,11 +444,16 @@
         for q in range(NQ):
             for s in (1, -1):
                 for d in PARENT:
-                    rs_copy(it, q, s, d).wait_send()
                     ag_copy(it, q, s, d).wait_send()
+                    if d in LEAVES:
+                        ag_copy(it, q, s, d, True).wait_send()
+                        rs_leaf(it, q, s, d, False).wait_send()
+                        rs_leaf(it, q, s, d, True).wait_send()
+                    else:
+                        rs_copy(it, q, s, d).wait_send()
             for n in range(len(GROUPS)):
                 sib_ag(it, q, n, own(q)).wait_send()
-            for n in range(len(PARTS)):
+            for n in range(2):
                 sib_rs(it, q, n).wait_send()
 
         for q in range(NQ):
@@ -522,14 +562,15 @@
             pltpu.VMEM((ITERS, NQ, CB, H, T), f32),
             pltpu.VMEM((ITERS, NQ, 2, 8, H, T), f32),
             pltpu.VMEM((ITERS, NQ, 2, 8, H, T), f32),
+            pltpu.VMEM((ITERS, NQ, 2, 8, H, T), f32),
             pltpu.VMEM((ITERS, RB, S, T), f32),
             pltpu.VMEM((ITERS, NQ, 2, 3, 2, H, T), f32),
             pltpu.VMEM((ITERS, NQ, 2, 2, H, T), f32),
             pltpu.VMEM((ITERS, NQ, 2, 3, FR, T), f32),
             pltpu.VMEM((2, S, T), f32),
             dma((8,)),
-            dma((ITERS, 2, NQ, 2, 8)),
-            dma((ITERS, 2, NQ, 2, 8)),
+            dma((ITERS, 4, NQ, 2, 8)),
+            dma((ITERS, 4, NQ, 2, 8)),
             dma((ITERS, 2, NQ, 4)),
             dma((ITERS, 2, NQ, 4)),
             dma((ITERS, NQ, 2, 4, 3)),

time: 116 us -> 114 us (0.983)
  Pallas kernels: 110 us -> 108 us
    pallas_call x1, Pallas kernels: 110 us -> 108 us  [per_device(): pl.pallas_call(kernel, out_shape=(jax.ShapeDtypeStruct((CB, T, S), f32),...]
where the time goes in v5:
time: 114 us; the launch traced here: 113 us
  Pallas kernels  108 us (95%)
  local copies, waits for them, and re-layouts  3.15 us (3%)
  other arithmetic  1.28 us (1%)
    pallas_call x1, Pallas kernels, per_device(): pl.pallas_call(kernel, out_shape=(jax.ShapeDtypeStruct((CB, T, S), f32),...  108 us
    unnamed x4, local copies, waits for them, and re-layouts  3.15 us

profile of v5, /device:TPU:1, one launch (start us, length us, event | category | flops | bytes accessed | tf_op | source)
XLA Modules:
  0.0 113.3 jit_solution(12916727724987766419)
XLA Ops:
  0.6 0.7 compare_select_fusion
  1.3 0.6 select_reduce_fusion.inv_ref
  1.9 108.2 %shard_map.104 = (f32[16,128,128]{2,1,0:T(8,128)}, f32[8,128,128]{2,1,0:T(8,128)}) custom-call(s32[128]{0:T(128)} %select_reduce_fusion.inv_ref, bf16[48,128,128]{2,1,0:T(8,128)(2,1)} %tiles_hbm.1, f32[16,128]{1,0:T(8,128)} %cost_hbm.1, f32[16,128]{1,0:T(8,128)} %cap_hbm.1, f32[8,128,128]{2,1,0:T(8,128)} %demand_hbm.1, s32[8,128]{1,0:T(8,128)} %kind_hbm.1, ...), custom_call_target="tpu_custom_call" | custom-call | flops 805306368 | bytes 6291456 | tf_op jit(solution)/shard_map/pallas_call | solution.py:539
  110.2 0.0 copy-start
  110.2 2.4 %copy.13 = f32[16,128,128]{2,1,0:T(8,128)} copy(f32[16,128,128]{2,1,0:T(8,128)} %get-tuple-element.4) | data formatting | bytes 2097152
  112.5 0.0 copy-done
  112.5 0.8 copy.14
Async XLA Ops:
  110.2 2.4 %copy-start = (f32[8,128,128]{2,1,0:T(8,128)S(1)}, f32[8,128,128]{2,1,0:T(8,128)}, u32[]{:S(2)}) copy-start(f32[8,128,128]{2,1,0:T(8,128)} %get-tuple-element.5) | copy-start | bytes 1572868

commit v6 on v5

--- a/solution.py
+++ b/solution.py
@@ -11,7 +11,7 @@
 NQ = 2
 SQ = S // NQ
 H = SQ // 2
-FR = H // 2
+FR = SQ // 2
 SLOTS = 48
 
 PARENT = {1: 0, 4: 0, 2: 1, 5: 4, 7: 4, 3: 2, 6: 5, 8: 7}
@@ -24,6 +24,11 @@
 LEAVES = LEVELS[3]
 LEAF_HOPS = sorted({s * (d - PARENT[d]) for d in LEAVES for s in (1, -1)})
 HOPS = sorted({s * (d - u) for d, u in PARENT.items() for s in (1, -1)})
+
+PLANE = sorted(
+    [(a, b) for a in range(NX) for b in range(NY) if a or b],
+    key=lambda o: -(min(o[0], NX - o[0]) + min(o[1], NY - o[1])),
+)
 
 primal_step = 0.5
 dual_step = 0.5
@@ -69,8 +74,6 @@
     rs_x,
     fp,
     rx,
-    g,
-    ry,
     dem,
     local_sem,
     ring_send,
@@ -84,8 +87,6 @@
     row = lax.axis_index("row")
     x, y = lax.div(col, NY), lax.rem(col, NY)
     z, core = lax.div(row, 2), lax.rem(row, 2)
-    outer = (x, y)
-    inner = (y, x)
     own_at = [pl.multiple_of(q * SQ + core * H, H) for q in range(NQ)]
     oth_at = [pl.multiple_of(q * SQ + (1 - core) * H, H) for q in range(NQ)]
     block_of = [lax.rem(z + OFFS[p] + NZ, NZ) for p in range(CB)]
@@ -94,9 +95,10 @@
     sibling = (col, z * 2 + 1 - core)
     x_at = [lax.rem(x + d, NX) for d in range(NX)]
     y_at = [lax.rem(y + d, NY) for d in range(NY)]
-    outer_at, inner_at = (x_at, y_at), (y_at, x_at)
-    x_col = [x_at[d] * NY + y for d in range(NX)]
-    y_col = [x * NY + y_at[d] for d in range(NY)]
+    plane_at = {
+        (a, b): x_at[a] * NY + y_at[b] for a in range(NX) for b in range(NY)
+    }
+    block_own = lax.div(col, 2)
 
     def own(q):
         return own_at[q]
@@ -110,17 +112,6 @@
     def zdev(d):
         return (col, z_row[d])
 
-    def xdev(d):
-        return (x_col[d], row)
-
-    def ydev(d):
-        return (y_col[d], row)
-
-    def sub(k):
-        return lax.div(k, 2), pl.multiple_of(lax.rem(k, 2) * FR, FR)
-
-    sub_at = [[sub(inner_at[h][d]) for d in range(4)] for h in range(2)]
-    dem_block = [2 * outer[h] + sub_at[h][0][0] for h in range(2)]
     loads = [
         pltpu.make_async_copy(src, dst, local_sem.at[n])
         for n, (src, dst) in enumerate(
@@ -131,8 +122,7 @@
                 (cost_hbm, cost),
                 (cap_hbm, cap),
                 (kind_hbm, kind),
-                (demand_hbm.at[dem_block[0]], dem0.at[0]),
-                (demand_hbm.at[dem_block[1]], dem0.at[1]),
+                (demand_hbm.at[block_own], dem0),
             ]
         )
     ]
@@ -142,7 +132,7 @@
     barrier = pltpu.get_barrier_semaphore()
     peers = [zdev(d) for d in HOPS] + [sibling]
     peers += [(col, cross_row[d]) for d in LEAF_HOPS]
-    peers += [xdev(d) for d in (1, 2, 3)] + [ydev(d) for d in (1, 2, 3)]
+    peers += [(plane_at[o], row) for o in PLANE]
     for peer in peers:
         pl.semaphore_signal(
             barrier, inc=1, device_id=peer, device_id_type=pl.DeviceIdType.MESH
@@ -213,46 +203,38 @@
             part, part, sib_send.at[it, 1, q, n], sib_recv.at[it, 1, q, n], sibling
         )
 
-    def f_dev(h, d, first):
-        return xdev(d) if (h == 0) == first else ydev(d)
-
-    def f_sem(it, q, h, phase, d):
-        i = (it, q, h, phase, d - 1)
-        return f_send.at[i], f_recv.at[i]
-
-    def f_rs1(it, q, h, d):
-        dest = outer_at[h][d]
-        return remote(
-            fp.at[it, pl.ds(2 * dest, 2), pl.ds(q * SQ + h * H, H), :],
-            rx.at[it, q, h, d - 1], *f_sem(it, q, h, 0, d), f_dev(h, d, True),
-        )
-
-    def f_rs2(it, q, h, d):
-        b, s0 = sub_at[h][d]
-        return remote(
-            g.at[it, q, h, b, pl.ds(s0, FR), :], ry.at[it, q, h, d - 1],
-            *f_sem(it, q, h, 1, d), f_dev(h, d, False),
-        )
-
-    def f_rows(q, h, s0):
-        return pl.ds(pl.multiple_of(q * SQ + h * H + s0, FR), FR)
-
-    def f_ag1(it, q, h, d, k):
-        b, s0 = sub_at[h][k]
-        part = dt.at[it + 1, 2 * outer[h] + b, f_rows(q, h, s0), :]
-        return remote(part, part, *f_sem(it, q, h, 2, d), f_dev(h, d, False))
-
-    def f_ag2(it, q, h, d, k):
-        part = dt.at[it + 1, pl.ds(2 * outer_at[h][k], 2), pl.ds(q * SQ + h * H, H), :]
-        return remote(part, part, *f_sem(it, q, h, 3, d), f_dev(h, d, True))
-
-    far_first = (2, 1, 3)
+    def chunk(q, k):
+        return lax.div(k, 2), pl.ds(
+            pl.multiple_of(q * SQ + lax.rem(k, 2) * FR, FR), FR
+        )
+
+    def back(o):
+        return (NX - o[0]) % NX, (NY - o[1]) % NY
+
+    def f_rs(it, q, j):
+        k = plane_at[PLANE[j]]
+        block, rows = chunk(q, k)
+        return remote(
+            fp.at[it, block, rows, :], rx.at[it, q, j],
+            f_send.at[it, q, 0, j], f_recv.at[it, q, 0, j], (k, row),
+        )
+
+    def f_ag(it, q, j, arrival=False):
+        block, rows = chunk(q, plane_at[back(PLANE[j])] if arrival else col)
+        part = dt.at[it + 1, block, rows, :]
+        return remote(
+            part, part, f_send.at[it, q, 1, j], f_recv.at[it, q, 1, j],
+            (plane_at[PLANE[j]], row),
+        )
+
+    others = range(len(PLANE))
+    near_first = tuple(reversed(others))
 
     def build(lo, hi):
         def rows_of(r, _):
             r0 = pl.multiple_of(r * T, T)
             for p in range(lo, hi):
-                idx = inv_ref[r * CB + block_at(p)]
+                idx = inv_ref[r, block_at(p)]
                 tile = tiles[jnp.maximum(idx, 0)]
                 tile = jnp.where(idx >= 0, tile, jnp.zeros_like(tile))
                 kd[pl.ds(r0, T), p * T : (p + 1) * T] = tile
@@ -260,17 +242,15 @@
 
         lax.fori_loop(0, RB, rows_of, 0)
 
-    def f_ag2_wait(it, q):
-        for h in range(2):
-            for d in (1, 2, 3):
-                f_ag2(it, q, h, d, 4 - d).wait_recv()
+    def f_ag_wait(it, q):
+        for j in near_first:
+            f_ag(it, q, j, True).wait_recv()
 
     def slab(q):
         return (q * SQ, SQ)
 
     def iteration(it, _):
-        def adjoint(n, rows):
-            lo, hi = PARTS[n]
+        def adjoint(lo, hi, rows):
             r0, many = rows
             for p in range(lo, hi, 2):
                 w = min(2, hi - p)
@@ -324,27 +304,28 @@
         def _():
             loads[0].wait()
             for b in range(RB):
-                dt[0, b] = dual0[b].T
+                dl[:, b * T : (b + 1) * T] = dual0[b].astype(jnp.bfloat16).T
             loads[1].wait()
             build(*PARTS[2])
             pl.semaphore_wait(barrier, len(peers))
 
         def partial(q, n):
-            adjoint(n, slab(q))
+            adjoint(*PARTS[n], slab(q))
             sib_rs(it, q, n).start()
 
         def begin(q):
             @pl.when(it > 0)
             def _():
-                f_ag2_wait(it - 1, q)
-
-            r0, many = slab(q)
-            for b in range(RB):
-                dl[r0 : r0 + many, b * T : (b + 1) * T] = dt[
-                    it, b, r0 : r0 + many
-                ].astype(jnp.bfloat16)
-            adjoint(2, slab(q))
+                f_ag_wait(it - 1, q)
+                r0, many = slab(q)
+                for b in range(RB):
+                    dl[r0 : r0 + many, b * T : (b + 1) * T] = dt[
+                        it, b, r0 : r0 + many
+                    ].astype(jnp.bfloat16)
+
             for d in LEAVES:
+                at = sorted({POS[d], POS[-d]})
+                adjoint(at[0], at[-1] + 1, slab(q))
                 for s in (1, -1):
                     rs_leaf(it, q, s, d, False).start()
                     rs_leaf(it, q, s, d, True).start()
@@ -366,8 +347,9 @@
                 load.wait()
             for p in range(CB):
                 pt[0, p] = primal0[block_at(p)].T
-            for h in range(2):
-                dem[h] = dem0[h].T
+            for b in range(RB):
+                dt[0, b] = dual0[b].T
+            dem[...] = dem0[...].T
 
         for q in range(NQ):
             rs_level(1, q)
@@ -432,9 +414,8 @@
                     ag_copy(it, q, s, d).wait_recv()
                     ag_copy(it, q, s, d, True, True).wait_recv()
             forward(11, 16, slab(q), False)
-            for d in far_first:
-                for h in range(2):
-                    f_rs1(it, q, h, d).start()
+            for j in others:
+                f_rs(it, q, j).start()
 
         @pl.when(it == ITERS - 1)
         def _():
@@ -457,65 +438,31 @@
                 sib_rs(it, q, n).wait_send()
 
         for q in range(NQ):
-            for h in range(2):
-                for d in (1, 3, 2):
-                    f_rs1(it, q, h, d).wait_recv()
-                for b in range(2):
-                    g[it, q, h, b] = (
-                        fp[it, 2 * outer[h] + b, q * SQ + h * H : q * SQ + (h + 1) * H]
-                        + rx[it, q, h, 0, b]
-                        + rx[it, q, h, 1, b]
-                        + rx[it, q, h, 2, b]
-                    )
-                for d in far_first:
-                    f_rs2(it, q, h, d).start()
-        for q in range(NQ):
-            for h in range(2):
-                for d in (1, 3, 2):
-                    f_rs2(it, q, h, d).wait_recv()
-                b, s0 = sub_at[h][0]
-                forward_sum = (
-                    g[it, q, h, b, pl.ds(s0, FR), :]
-                    + ry[it, q, h, 0]
-                    + ry[it, q, h, 1]
-                    + ry[it, q, h, 2]
-                )
-                block = 2 * outer[h] + b
-                rows = f_rows(q, h, s0)
-                new = dt[it, block, rows, :] + dual_step * (
-                    dem[h, rows, :] - forward_sum
-                )
-                new = jnp.where(
-                    kind[pl.ds(block, 1), :] == 1, jnp.maximum(new, 0.0), new
-                )
-                dt[it + 1, block, rows, :] = new
-                for d in far_first:
-                    f_ag1(it, q, h, d, 0).start()
-        for q in range(NQ):
-            for h in range(2):
-                for d in (1, 3, 2):
-                    f_ag1(it, q, h, d, 4 - d).wait_recv()
-                for d in far_first:
-                    f_ag2(it, q, h, d, 0).start()
-        for q in range(NQ):
-            for h in range(2):
-                for d in (1, 2, 3):
-                    f_rs1(it, q, h, d).wait_send()
-                    f_rs2(it, q, h, d).wait_send()
-                    f_ag1(it, q, h, d, 0).wait_send()
+            block, rows = chunk(q, col)
+            forward_sum = fp[it, block, rows, :]
+            for j in near_first:
+                f_rs(it, q, j).wait_recv()
+                forward_sum = forward_sum + rx[it, q, j]
+            new = dt[it, block, rows, :] + dual_step * (dem[rows, :] - forward_sum)
+            new = jnp.where(kind[pl.ds(block, 1), :] == 1, jnp.maximum(new, 0.0), new)
+            dt[it + 1, block, rows, :] = new
+            for j in others:
+                f_ag(it, q, j).start()
+        for q in range(NQ):
+            for j in others:
+                f_rs(it, q, j).wait_send()
         return 0
 
     lax.fori_loop(0, ITERS, iteration, 0)
     for q in range(NQ):
-        f_ag2_wait(ITERS - 1, q)
+        f_ag_wait(ITERS - 1, q)
     for b in range(RB):
         dual_out[b] = dt[ITERS, b].T
 
     for it in range(ITERS):
         for q in range(NQ):
-            for h in range(2):
-                for d in (1, 2, 3):
-                    f_ag2(it, q, h, d, 0).wait_send()
+            for j in others:
+                f_ag(it, q, j).wait_send()
 
 
 def per_device(
@@ -529,10 +476,11 @@
     primal_start,
     dual_start,
 ):
-    place = jnp.where(tile_row < RB, tile_row * CB + tile_column, RB * CB)
-    slot = jnp.arange(SLOTS, dtype=jnp.int32)
-    hit = place[:, None] == jnp.arange(RB * CB, dtype=jnp.int32)[None, :]
-    inv = jnp.max(jnp.where(hit, slot[:, None], -1), axis=0)
+    dims = (SLOTS, RB, CB)
+    hit = (tile_row[:, None, None] == lax.broadcasted_iota(jnp.int32, dims, 1)) & (
+        tile_column[:, None, None] == lax.broadcasted_iota(jnp.int32, dims, 2)
+    )
+    inv = jnp.max(jnp.where(hit, lax.broadcasted_iota(jnp.int32, dims, 0), -1), axis=0)
     vmem = pl.BlockSpec(memory_space=pltpu.VMEM)
     f32, bf16 = jnp.float32, jnp.bfloat16
     dma = pltpu.SemaphoreType.DMA
@@ -552,7 +500,7 @@
             pltpu.VMEM((RB, T), jnp.int32),
             pltpu.VMEM((CB, T, S), f32),
             pltpu.VMEM((RB, T, S), f32),
-            pltpu.VMEM((2, T, S), f32),
+            pltpu.VMEM((T, S), f32),
             pltpu.VMEM((RB * T, CB * T), bf16),
             pltpu.VMEM((ITERS + 1, CB, S, T), f32),
             pltpu.VMEM((ITERS + 1, RB, S, T), f32),
@@ -564,17 +512,15 @@
             pltpu.VMEM((ITERS, NQ, 2, 8, H, T), f32),
             pltpu.VMEM((ITERS, NQ, 2, 8, H, T), f32),
             pltpu.VMEM((ITERS, RB, S, T), f32),
-            pltpu.VMEM((ITERS, NQ, 2, 3, 2, H, T), f32),
-            pltpu.VMEM((ITERS, NQ, 2, 2, H, T), f32),
-            pltpu.VMEM((ITERS, NQ, 2, 3, FR, T), f32),
-            pltpu.VMEM((2, S, T), f32),
-            dma((8,)),
+            pltpu.VMEM((ITERS, NQ, len(PLANE), FR, T), f32),
+            pltpu.VMEM((S, T), f32),
+            dma((7,)),
             dma((ITERS, 4, NQ, 2, 8)),
             dma((ITERS, 4, NQ, 2, 8)),
             dma((ITERS, 2, NQ, 4)),
             dma((ITERS, 2, NQ, 4)),
-            dma((ITERS, NQ, 2, 4, 3)),
-            dma((ITERS, NQ, 2, 4, 3)),
+            dma((ITERS, NQ, 2, len(PLANE))),
+            dma((ITERS, NQ, 2, len(PLANE))),
         ],
         compiler_params=pltpu.CompilerParams(
             collective_id=0, has_side_effects=True, vmem_limit_bytes=56 << 20

time: 114 us -> 112 us (0.982)
    pallas_call x1, Pallas kernels: 108 us -> 107 us  [per_device(): pl.pallas_call(kernel, out_shape=(jax.ShapeDtypeStruct((CB, T, S), f32),...]
where the time goes in v6:
time: 112 us
  Pallas kernels  107 us (96%)
  local copies, waits for them, and re-layouts  3.15 us (3%)
  other arithmetic  1.48 us (1%)
    pallas_call x1, Pallas kernels, per_device(): pl.pallas_call(kernel, out_shape=(jax.ShapeDtypeStruct((CB, T, S), f32),...  107 us
    unnamed x4, local copies, waits for them, and re-layouts  3.15 us

profile of v6, /device:TPU:1, one launch (start us, length us, event | category | flops | bytes accessed | tf_op | source)
XLA Modules:
  0.0 112.0 jit_solution(18414195028978985749)
XLA Ops:
  0.6 1.5 %select_reduce_fusion.inv_ref = s32[8,16]{1,0:T(8,128)} fusion(s32[48]{0:T(128)} %param.11, s32[48]{0:T(128)} %param.10), kind=kLoop, calls=%fused_computation | loop fusion | flops 30592 | bytes 896 | tf_op jit(solution)/shard_map/reduce_max | solution.py:483
  2.1 106.7 %shard_map.104 = (f32[16,128,128]{2,1,0:T(8,128)}, f32[8,128,128]{2,1,0:T(8,128)}) custom-call(s32[8,16]{1,0:T(8,128)} %select_reduce_fusion.inv_ref, bf16[48,128,128]{2,1,0:T(8,128)(2,1)} %tiles_hbm.1, f32[16,128]{1,0:T(8,128)} %cost_hbm.1, f32[16,128]{1,0:T(8,128)} %cap_hbm.1, f32[8,128,128]{2,1,0:T(8,128)} %demand_hbm.1, s32[8,128]{1,0:T(8,128)} %kind_hbm.1, ...), custom_call_target="tpu_custom_call" | custom-call | flops 805306368 | bytes 6291456 | tf_op jit(solution)/shard_map/pallas_call | solution.py:487
  108.9 0.0 copy-start
  108.9 2.4 %copy.13 = f32[16,128,128]{2,1,0:T(8,128)} copy(f32[16,128,128]{2,1,0:T(8,128)} %get-tuple-element.4) | data formatting | bytes 2097152
  111.2 0.0 copy-done
  111.2 0.8 copy.14
Async XLA Ops:
  108.9 2.4 %copy-start = (f32[8,128,128]{2,1,0:T(8,128)S(1)}, f32[8,128,128]{2,1,0:T(8,128)}, u32[]{:S(2)}) copy-start(f32[8,128,128]{2,1,0:T(8,128)} %get-tuple-element.5) | copy-start | bytes 1572868

commit v7 on v6

--- a/solution.py
+++ b/solution.py
@@ -14,15 +14,14 @@
 FR = SQ // 2
 SLOTS = 48
 
-PARENT = {1: 0, 4: 0, 2: 1, 5: 4, 7: 4, 3: 2, 6: 5, 8: 7}
-LEVELS = ((0,), (4, 1), (7, 5, 2), (8, 6, 3))
-OFFS = (0, 1, -1, 4, -4, 2, -2, 5, -5, 7, -7, 3, -3, 6, -6, 8)
+PARENT = {1: 0, 3: 0, 6: 0, 2: 3, 4: 3, 5: 6, 7: 6, 8: 6}
+HEADS = (6, 3, 1)
+OFFS = (0, 1, -1, 3, -3, 6, -6, 2, -2, 4, -4, 5, -5, 7, -7, 8)
 POS = {o: p for p, o in enumerate(OFFS)}
 POS[-8] = POS[8]
-PARTS = ((0, 5), (5, 11), (11, 16))
-GROUPS = ((0, 1), (1, 5), (5, 11))
-LEAVES = LEVELS[3]
-LEAF_HOPS = sorted({s * (d - PARENT[d]) for d in LEAVES for s in (1, -1)})
+PARTS = ((0, 7), (7, 11), (11, 16))
+GROUPS = ((0, 1), (1, 7), (7, 11), (11, 16))
+LEAVES = {1: (4, 2), 2: (8, 7, 5)}
 HOPS = sorted({s * (d - u) for d, u in PARENT.items() for s in (1, -1)})
 
 PLANE = sorted(
@@ -71,7 +70,6 @@
     sib,
     rs_s,
     rs_r,
-    rs_x,
     fp,
     rx,
     dem,
@@ -91,7 +89,6 @@
     oth_at = [pl.multiple_of(q * SQ + (1 - core) * H, H) for q in range(NQ)]
     block_of = [lax.rem(z + OFFS[p] + NZ, NZ) for p in range(CB)]
     z_row = {d: lax.rem(z + d + NZ, NZ) * 2 + core for d in HOPS}
-    cross_row = {d: lax.rem(z + d + NZ, NZ) * 2 + 1 - core for d in LEAF_HOPS}
     sibling = (col, z * 2 + 1 - core)
     x_at = [lax.rem(x + d, NX) for d in range(NX)]
     y_at = [lax.rem(y + d, NY) for d in range(NY)]
@@ -131,7 +128,6 @@
 
     barrier = pltpu.get_barrier_semaphore()
     peers = [zdev(d) for d in HOPS] + [sibling]
-    peers += [(col, cross_row[d]) for d in LEAF_HOPS]
     peers += [(plane_at[o], row) for o in PLANE]
     for peer in peers:
         pl.semaphore_signal(
@@ -158,35 +154,17 @@
             ring_recv.at[it, 0, q, side(s), d - 1], zdev(s * (d - PARENT[d])),
         )
 
-    def rows_at(first, s, d):
+    def own_rows(q, s, d):
         start, size = half(s, d)
-        return pl.ds(pl.multiple_of(first + start, 16), size)
-
-    def own_rows(q, s, d):
-        return rows_at(own(q), s, d)
-
-    def rs_leaf(it, q, s, d, cross):
-        hop = s * (d - PARENT[d])
-        phase, into = (2, rs_x) if cross else (0, rs_r)
-        rows = rows_at(oth(q) if cross else own(q), s, d)
-        return remote(
-            ap.at[it, POS[s * d], rows, :],
-            into.at[it, q, side(s), d - 1, pl.ds(0, half(s, d)[1])],
-            ring_send.at[it, phase, q, side(s), d - 1],
-            ring_recv.at[it, phase, q, side(s), d - 1],
-            (col, cross_row[hop] if cross else z_row[hop]),
-        )
-
-    def ag_copy(it, q, s, d, cross=False, arrival=False):
-        hop = s * (d - PARENT[d])
-        phase = 3 if cross else 1
-        rows = rows_at(oth(q) if cross and arrival else own(q), s, d)
+        return pl.ds(pl.multiple_of(own(q) + start, 16), size)
+
+    def ag_copy(it, q, s, d):
+        rows = own_rows(q, s, d)
         return remote(
             pt.at[it + 1, POS[-s * PARENT[d]], rows, :],
             pt.at[it + 1, POS[-s * d], rows, :],
-            ring_send.at[it, phase, q, side(s), d - 1],
-            ring_recv.at[it, phase, q, side(s), d - 1],
-            (col, cross_row[hop] if cross else z_row[hop]),
+            ring_send.at[it, 1, q, side(s), d - 1],
+            ring_recv.at[it, 1, q, side(s), d - 1], zdev(s * (d - PARENT[d])),
         )
 
     def sib_rs(it, q, n):
@@ -234,7 +212,7 @@
         def rows_of(r, _):
             r0 = pl.multiple_of(r * T, T)
             for p in range(lo, hi):
-                idx = inv_ref[r, block_at(p)]
+                idx = inv_ref[r * CB + block_at(p)]
                 tile = tiles[jnp.maximum(idx, 0)]
                 tile = jnp.where(idx >= 0, tile, jnp.zeros_like(tile))
                 kd[pl.ds(r0, T), p * T : (p + 1) * T] = tile
@@ -274,15 +252,9 @@
                 ap[it, p, own_rows(q, s, d), :] + sib[it, q, p, start : start + size, :]
             )
             for c in children(d):
-                if c in LEAVES:
-                    rs_leaf(it, q, s, c, False).wait_recv()
-                    rs_leaf(it, q, s, c, True).wait_recv()
-                else:
-                    rs_copy(it, q, s, c).wait_recv()
+                rs_copy(it, q, s, c).wait_recv()
                 if c != 8:
                     value = value + rs_r[it, q, side(s), c - 1]
-                if c in (3, 6):
-                    value = value + rs_x[it, q, side(s), c - 1]
             rs_s[it, q, side(s), d - 1, :size] = value
             if 8 in children(d):
                 at, many = half(s, 8)
@@ -290,13 +262,12 @@
                 rs_s[it, q, side(s), d - 1, rows] = (
                     rs_s[it, q, side(s), d - 1, rows]
                     + rs_r[it, q, side(s), 7, :many]
-                    + rs_x[it, q, side(s), 7, :many]
                 )
             rs_copy(it, q, s, d).start()
 
-        def rs_level(n, q):
-            sib_rs(it, q, n - 1).wait_recv()
-            for d in LEVELS[n]:
+        def rs_part(n, q):
+            sib_rs(it, q, n).wait_recv()
+            for d in HEADS if n == 0 else LEAVES[n]:
                 for s in (1, -1):
                     rs_node(q, s, d)
 
@@ -306,7 +277,7 @@
             for b in range(RB):
                 dl[:, b * T : (b + 1) * T] = dual0[b].astype(jnp.bfloat16).T
             loads[1].wait()
-            build(*PARTS[2])
+            build(PARTS[1][0], PARTS[2][1])
             pl.semaphore_wait(barrier, len(peers))
 
         def partial(q, n):
@@ -323,23 +294,18 @@
                         it, b, r0 : r0 + many
                     ].astype(jnp.bfloat16)
 
-            for d in LEAVES:
-                at = sorted({POS[d], POS[-d]})
-                adjoint(at[0], at[-1] + 1, slab(q))
-                for s in (1, -1):
-                    rs_leaf(it, q, s, d, False).start()
-                    rs_leaf(it, q, s, d, True).start()
+            partial(q, 2)
+            partial(q, 1)
 
         begin(0)
-        build_first(1)
-        partial(0, 1)
-        begin(1)
-        partial(1, 1)
         build_first(0)
         partial(0, 0)
+        rs_part(2, 0)
+        rs_part(1, 0)
+        begin(1)
         partial(1, 0)
-        for q in range(NQ):
-            rs_level(2, q)
+        rs_part(2, 1)
+        rs_part(1, 1)
 
         @pl.when(it == 0)
         def _():
@@ -352,12 +318,12 @@
             dem[...] = dem0[...].T
 
         for q in range(NQ):
-            rs_level(1, q)
+            rs_part(0, q)
 
         for q in range(NQ):
             rows = pl.ds(own(q), H)
             total = ap[it, 0, rows, :] + sib[it, q, 0]
-            for d in reversed(LEVELS[1]):
+            for d in reversed(HEADS):
                 for s in (1, -1):
                     rs_copy(it, q, s, d).wait_recv()
                     total = total + rs_r[it, q, side(s), d - 1]
@@ -366,20 +332,25 @@
                 jnp.maximum(old - primal_step * (cost[pl.ds(z, 1), :] - total), 0.0),
                 cap[pl.ds(z, 1), :],
             )
-            for d in LEVELS[1]:
+            for d in HEADS:
                 for s in (1, -1):
                     ag_copy(it, q, s, d).start()
             sib_ag(it, q, 0, own(q)).start()
 
-        def ag_level(n, q):
-            for d in reversed(LEVELS[n]):
+        def ag_heads(q):
+            for d in HEADS:
                 for s in (1, -1):
                     ag_copy(it, q, s, d).wait_recv()
                     for c in reversed(children(d)):
                         ag_copy(it, q, s, c).start()
-                        if c in LEAVES:
-                            ag_copy(it, q, s, c, True).start()
-            sib_ag(it, q, n, own(q)).start()
+            sib_ag(it, q, 1, own(q)).start()
+
+        def ag_leaves(q):
+            for n in (2, 1):
+                for d in LEAVES[n]:
+                    for s in (1, -1):
+                        ag_copy(it, q, s, d).wait_recv()
+                sib_ag(it, q, n + 1, own(q)).start()
 
         def forward(lo, hi, rows, first):
             r0, many = rows
@@ -399,23 +370,26 @@
                     part = res[:, k * T : (k + 1) * T]
                     fp[it, n + k, at] = part if first else fp[it, n + k, at] + part
 
-        for n in (1, 2):
-            for q in range(NQ):
-                ag_level(n, q)
-        for q in range(NQ):
+        def forward_heads(q):
             sib_ag(it, q, 0, oth(q)).wait_recv()
             sib_ag(it, q, 1, oth(q)).wait_recv()
-            forward(0, 5, slab(q), True)
-        for q in range(NQ):
+            forward(0, 7, slab(q), True)
+
+        def forward_leaves(q):
+            sib_ag(it, q, 3, oth(q)).wait_recv()
             sib_ag(it, q, 2, oth(q)).wait_recv()
-            forward(5, 11, slab(q), False)
-            for d in LEAVES:
-                for s in (1, -1):
-                    ag_copy(it, q, s, d).wait_recv()
-                    ag_copy(it, q, s, d, True, True).wait_recv()
-            forward(11, 16, slab(q), False)
+            forward(7, 16, slab(q), False)
             for j in others:
                 f_rs(it, q, j).start()
+
+        ag_heads(0)
+        ag_heads(1)
+        forward_heads(0)
+        ag_leaves(0)
+        forward_heads(1)
+        forward_leaves(0)
+        ag_leaves(1)
+        forward_leaves(1)
 
         @pl.when(it == ITERS - 1)
         def _():
@@ -426,15 +400,10 @@
             for s in (1, -1):
                 for d in PARENT:
                     ag_copy(it, q, s, d).wait_send()
-                    if d in LEAVES:
-                        ag_copy(it, q, s, d, True).wait_send()
-                        rs_leaf(it, q, s, d, False).wait_send()
-                        rs_leaf(it, q, s, d, True).wait_send()
-                    else:
-                        rs_copy(it, q, s, d).wait_send()
+                    rs_copy(it, q, s, d).wait_send()
             for n in range(len(GROUPS)):
                 sib_ag(it, q, n, own(q)).wait_send()
-            for n in range(2):
+            for n in range(len(PARTS)):
                 sib_rs(it, q, n).wait_send()
 
         for q in range(NQ):
@@ -476,11 +445,10 @@
     primal_start,
     dual_start,
 ):
-    dims = (SLOTS, RB, CB)
-    hit = (tile_row[:, None, None] == lax.broadcasted_iota(jnp.int32, dims, 1)) & (
-        tile_column[:, None, None] == lax.broadcasted_iota(jnp.int32, dims, 2)
-    )
-    inv = jnp.max(jnp.where(hit, lax.broadcasted_iota(jnp.int32, dims, 0), -1), axis=0)
+    place = jnp.where(tile_row < RB, tile_row * CB + tile_column, RB * CB)
+    slot = jnp.arange(SLOTS, dtype=jnp.int32)
+    hit = place[:, None] == jnp.arange(RB * CB, dtype=jnp.int32)[None, :]
+    inv = jnp.max(jnp.where(hit, slot[:, None], -1), axis=0)
     vmem = pl.BlockSpec(memory_space=pltpu.VMEM)
     f32, bf16 = jnp.float32, jnp.bfloat16
     dma = pltpu.SemaphoreType.DMA
@@ -510,13 +478,12 @@
             pltpu.VMEM((ITERS, NQ, CB, H, T), f32),
             pltpu.VMEM((ITERS, NQ, 2, 8, H, T), f32),
             pltpu.VMEM((ITERS, NQ, 2, 8, H, T), f32),
-            pltpu.VMEM((ITERS, NQ, 2, 8, H, T), f32),
             pltpu.VMEM((ITERS, RB, S, T), f32),
             pltpu.VMEM((ITERS, NQ, len(PLANE), FR, T), f32),
             pltpu.VMEM((S, T), f32),
             dma((7,)),
-            dma((ITERS, 4, NQ, 2, 8)),
-            dma((ITERS, 4, NQ, 2, 8)),
+            dma((ITERS, 2, NQ, 2, 8)),
+            dma((ITERS, 2, NQ, 2, 8)),
             dma((ITERS, 2, NQ, 4)),
             dma((ITERS, 2, NQ, 4)),
             dma((ITERS, NQ, 2, len(PLANE))),

time: 112 us -> 110 us (0.982)
  Pallas kernels: 107 us -> 104 us
    pallas_call x1, Pallas kernels: 107 us -> 104 us  [per_device(): pl.pallas_call(kernel, out_shape=(jax.ShapeDtypeStruct((CB, T, S), f32),...]
where the time goes in v7:
time: 110 us; the launch traced here: 109 us
  Pallas kernels  104 us (95%)
  local copies, waits for them, and re-layouts  3.15 us (3%)
  other arithmetic  1.28 us (1%)
    pallas_call x1, Pallas kernels, per_device(): pl.pallas_call(kernel, out_shape=(jax.ShapeDtypeStruct((CB, T, S), f32),...  104 us
    unnamed x4, local copies, waits for them, and re-layouts  3.15 us

profile of v7, /device:TPU:1, one launch (start us, length us, event | category | flops | bytes accessed | tf_op | source)
XLA Modules:
  0.0 109.5 jit_solution(12176744571500292265)
XLA Ops:
  0.6 0.7 compare_select_fusion
  1.3 0.6 select_reduce_fusion.inv_ref
  1.9 104.4 %shard_map.104 = (f32[16,128,128]{2,1,0:T(8,128)}, f32[8,128,128]{2,1,0:T(8,128)}) custom-call(s32[128]{0:T(128)} %select_reduce_fusion.inv_ref, bf16[48,128,128]{2,1,0:T(8,128)(2,1)} %tiles_hbm.1, f32[16,128]{1,0:T(8,128)} %cost_hbm.1, f32[16,128]{1,0:T(8,128)} %cap_hbm.1, f32[8,128,128]{2,1,0:T(8,128)} %demand_hbm.1, s32[8,128]{1,0:T(8,128)} %kind_hbm.1, ...), custom_call_target="tpu_custom_call" | custom-call | flops 805306368 | bytes 6291456 | tf_op jit(solution)/shard_map/pallas_call | solution.py:455
  106.3 0.0 copy-start
  106.3 2.4 %copy.13 = f32[16,128,128]{2,1,0:T(8,128)} copy(f32[16,128,128]{2,1,0:T(8,128)} %get-tuple-element.4) | data formatting | bytes 2097152
  108.7 0.0 copy-done
  108.7 0.8 copy.14
Async XLA Ops:
  106.3 2.4 %copy-start = (f32[8,128,128]{2,1,0:T(8,128)S(1)}, f32[8,128,128]{2,1,0:T(8,128)}, u32[]{:S(2)}) copy-start(f32[8,128,128]{2,1,0:T(8,128)} %get-tuple-element.5) | copy-start | bytes 1572868

commit v8 on v7

--- a/solution.py
+++ b/solution.py
@@ -72,8 +72,10 @@
     rs_r,
     fp,
     rx,
+    primal_t,
     dem,
     local_sem,
+    leave_sem,
     ring_send,
     ring_recv,
     sib_send,
@@ -224,6 +226,11 @@
         for j in near_first:
             f_ag(it, q, j, True).wait_recv()
 
+    def leave(p):
+        return pltpu.make_async_copy(
+            primal_t.at[p], primal_out.at[block_at(p)], leave_sem.at[p]
+        )
+
     def slab(q):
         return (q * SQ, SQ)
 
@@ -311,11 +318,7 @@
         def _():
             for load in loads[2:]:
                 load.wait()
-            for p in range(CB):
-                pt[0, p] = primal0[block_at(p)].T
-            for b in range(RB):
-                dt[0, b] = dual0[b].T
-            dem[...] = dem0[...].T
+            pt[0, 0] = primal0[block_at(0)].T
 
         for q in range(NQ):
             rs_part(0, q)
@@ -336,6 +339,14 @@
                 for s in (1, -1):
                     ag_copy(it, q, s, d).start()
             sib_ag(it, q, 0, own(q)).start()
+
+        @pl.when(it == 0)
+        def _():
+            for p in range(1, CB):
+                pt[0, p] = primal0[block_at(p)].T
+            for b in range(RB):
+                dt[0, b] = dual0[b].T
+            dem[...] = dem0[...].T
 
         def ag_heads(q):
             for d in HEADS:
@@ -394,7 +405,8 @@
         @pl.when(it == ITERS - 1)
         def _():
             for p in range(CB):
-                primal_out[block_at(p)] = pt[ITERS, p].T
+                primal_t[p] = pt[ITERS, p].T
+                leave(p).start()
 
         for q in range(NQ):
             for s in (1, -1):
@@ -427,11 +439,28 @@
         f_ag_wait(ITERS - 1, q)
     for b in range(RB):
         dual_out[b] = dt[ITERS, b].T
+    for p in range(CB):
+        leave(p).wait()
 
     for it in range(ITERS):
         for q in range(NQ):
             for j in others:
                 f_ag(it, q, j).wait_send()
+
+
+def hand_over(primal, dual, primal_out, dual_out, sem):
+    copies = []
+    for src, dst, blocks in ((primal, primal_out, CB), (dual, dual_out, RB)):
+        for b in range(0, blocks, 4):
+            copies.append(
+                pltpu.make_async_copy(
+                    src.at[b : b + 4], dst.at[b : b + 4], sem.at[len(copies)]
+                )
+            )
+    for copy in copies:
+        copy.start()
+    for copy in copies:
+        copy.wait()
 
 
 def per_device(
@@ -450,17 +479,19 @@
     hit = place[:, None] == jnp.arange(RB * CB, dtype=jnp.int32)[None, :]
     inv = jnp.max(jnp.where(hit, slot[:, None], -1), axis=0)
     vmem = pl.BlockSpec(memory_space=pltpu.VMEM)
+    hbm = pl.BlockSpec(memory_space=pl.ANY)
     f32, bf16 = jnp.float32, jnp.bfloat16
     dma = pltpu.SemaphoreType.DMA
-    return pl.pallas_call(
+    outs = (
+        jax.ShapeDtypeStruct((CB, T, S), f32),
+        jax.ShapeDtypeStruct((RB, T, S), f32),
+    )
+    results = pl.pallas_call(
         kernel,
-        out_shape=(
-            jax.ShapeDtypeStruct((CB, T, S), f32),
-            jax.ShapeDtypeStruct((RB, T, S), f32),
-        ),
+        out_shape=outs,
         in_specs=[pl.BlockSpec(memory_space=pltpu.SMEM)]
-        + [pl.BlockSpec(memory_space=pl.ANY)] * 7,
-        out_specs=(vmem, vmem),
+        + [hbm] * 7,
+        out_specs=(hbm, vmem),
         scratch_shapes=[
             pltpu.VMEM((SLOTS, T, T), bf16),
             pltpu.VMEM((CB, T), f32),
@@ -480,8 +511,10 @@
             pltpu.VMEM((ITERS, NQ, 2, 8, H, T), f32),
             pltpu.VMEM((ITERS, RB, S, T), f32),
             pltpu.VMEM((ITERS, NQ, len(PLANE), FR, T), f32),
+            pltpu.VMEM((CB, T, S), f32),
             pltpu.VMEM((S, T), f32),
             dma((7,)),
+            dma((CB,)),
             dma((ITERS, 2, NQ, 2, 8)),
             dma((ITERS, 2, NQ, 2, 8)),
             dma((ITERS, 2, NQ, 4)),
@@ -505,6 +538,14 @@
         primal_start,
         dual_start,
     )
+    return pl.pallas_call(
+        hand_over,
+        out_shape=outs,
+        in_specs=[hbm] * 2,
+        out_specs=(hbm, hbm),
+        scratch_shapes=[dma((CB // 4 + RB // 4,))],
+        compiler_params=pltpu.CompilerParams(vmem_limit_bytes=56 << 20),
+    )(*results)
 
 
 def solution(mesh):

time: 110 us -> 156 us (1.42)
  Pallas kernels: 104 us -> 153 us
  local copies, waits for them, and re-layouts: 3.15 us -> 0 us
    pallas_call x1 -> x2, Pallas kernels: 104 us -> 153 us  [the longest x1 105 us: per_device(): pl.pallas_call(kernel, out_shape=outs, in_specs=[pl.BlockSpec(memory_spac...]
    unnamed x4 -> x0, local copies, waits for them, and re-layouts: 3.15 us -> none
where the time goes in v8:
time: 156 us; the launch traced here: 155 us
  Pallas kernels  153 us (98%)
    pallas_call x1, Pallas kernels, per_device(): pl.pallas_call(kernel, out_shape=outs, in_specs=[pl.BlockSpec(memory_spac...  105 us
    pallas_call x1, Pallas kernels, per_device(): pl.pallas_call(hand_over, out_shape=outs, in_specs=[hbm] * 2, out_specs=(...  48.8 us

profile of v8, /device:TPU:1, one launch (start us, length us, event | category | flops | bytes accessed | tf_op | source)
XLA Modules:
  0.0 155.4 jit_solution(553061455115612297)
XLA Ops:
  0.6 0.7 compare_select_fusion
  1.3 0.6 select_reduce_fusion.inv_ref
  1.9 104.7 %shard_map.104 = (f32[16,128,128]{2,1,0:T(8,128)}, f32[8,128,128]{2,1,0:T(8,128)}) custom-call(s32[128]{0:T(128)} %select_reduce_fusion.inv_ref, bf16[48,128,128]{2,1,0:T(8,128)(2,1)} %tiles_hbm.1, f32[16,128]{1,0:T(8,128)} %cost_hbm.1, f32[16,128]{1,0:T(8,128)} %cap_hbm.1, f32[8,128,128]{2,1,0:T(8,128)} %demand_hbm.1, s32[8,128]{1,0:T(8,128)} %kind_hbm.1, ...), custom_call_target="tpu_custom_call" | custom-call | flops 805306368 | bytes 6291456 | tf_op jit(solution)/shard_map/pallas_call | solution.py:489
  106.6 48.8 %shard_map.105 = (f32[16,128,128]{2,1,0:T(8,128)}, f32[8,128,128]{2,1,0:T(8,128)}) custom-call(f32[16,128,128]{2,1,0:T(8,128)} %get-tuple-element.4.primal, f32[8,128,128]{2,1,0:T(8,128)} %get-tuple-element.5.dual), custom_call_target="tpu_custom_call" | custom-call | tf_op jit(solution)/shard_map/pallas_call | solution.py:541

commit v9 on v8

--- a/solution.py
+++ b/solution.py
@@ -448,18 +448,26 @@
                 f_ag(it, q, j).wait_send()
 
 
-def hand_over(primal, dual, primal_out, dual_out, sem):
-    copies = []
-    for src, dst, blocks in ((primal, primal_out, CB), (dual, dual_out, RB)):
+def hand_over(primal, dual, primal_out, dual_out, primal_v, dual_v, in_sem, out_sem):
+    arrive, leave = [], []
+    for src, mid, dst, blocks in (
+        (primal, primal_v, primal_out, CB),
+        (dual, dual_v, dual_out, RB),
+    ):
         for b in range(0, blocks, 4):
-            copies.append(
-                pltpu.make_async_copy(
-                    src.at[b : b + 4], dst.at[b : b + 4], sem.at[len(copies)]
-                )
+            n, part = len(arrive), slice(b, b + 4)
+            arrive.append(
+                pltpu.make_async_copy(src.at[part], mid.at[part], in_sem.at[n])
             )
-    for copy in copies:
+            leave.append(
+                pltpu.make_async_copy(mid.at[part], dst.at[part], out_sem.at[n])
+            )
+    for copy in arrive:
         copy.start()
-    for copy in copies:
+    for come, go in zip(arrive, leave):
+        come.wait()
+        go.start()
+    for copy in leave:
         copy.wait()
 
 
@@ -543,7 +551,12 @@
         out_shape=outs,
         in_specs=[hbm] * 2,
         out_specs=(hbm, hbm),
-        scratch_shapes=[dma((CB // 4 + RB // 4,))],
+        scratch_shapes=[
+            pltpu.VMEM((CB, T, S), f32),
+            pltpu.VMEM((RB, T, S), f32),
+            dma((CB // 4 + RB // 4,)),
+            dma((CB // 4 + RB // 4,)),
+        ],
         compiler_params=pltpu.CompilerParams(vmem_limit_bytes=56 << 20),
     )(*results)
 

time: 156 us -> 109 us (0.70)
  Pallas kernels: 153 us -> 107 us
    pallas_call x1, Pallas kernels: 48.8 us -> 2.19 us  [per_device(): pl.pallas_call(hand_over, out_shape=outs, in_specs=[hbm] * 2, out_specs=(...]
where the time goes in v9:
time: 109 us
  Pallas kernels  107 us (98%)
  other arithmetic  1.28 us (1%)
    pallas_call x1, Pallas kernels, per_device(): pl.pallas_call(kernel, out_shape=outs, in_specs=[pl.BlockSpec(memory_spac...  105 us
    pallas_call x1, Pallas kernels, per_device(): pl.pallas_call(hand_over, out_shape=outs, in_specs=[hbm] * 2, out_specs=(...  2.19 us

profile of v9, /device:TPU:1, one launch (start us, length us, event | category | flops | bytes accessed | tf_op | source)
XLA Modules:
  0.0 108.8 jit_solution(9647948802838174782)
XLA Ops:
  0.6 0.7 compare_select_fusion
  1.3 0.6 select_reduce_fusion.inv_ref
  1.9 104.7 %shard_map.104 = (f32[16,128,128]{2,1,0:T(8,128)}, f32[8,128,128]{2,1,0:T(8,128)}) custom-call(s32[128]{0:T(128)} %select_reduce_fusion.inv_ref, bf16[48,128,128]{2,1,0:T(8,128)(2,1)} %tiles_hbm.1, f32[16,128]{1,0:T(8,128)} %cost_hbm.1, f32[16,128]{1,0:T(8,128)} %cap_hbm.1, f32[8,128,128]{2,1,0:T(8,128)} %demand_hbm.1, s32[8,128]{1,0:T(8,128)} %kind_hbm.1, ...), custom_call_target="tpu_custom_call" | custom-call | flops 805306368 | bytes 6291456 | tf_op jit(solution)/shard_map/pallas_call | solution.py:497
  106.6 2.2 %shard_map.105 = (f32[16,128,128]{2,1,0:T(8,128)}, f32[8,128,128]{2,1,0:T(8,128)}) custom-call(f32[16,128,128]{2,1,0:T(8,128)} %get-tuple-element.4.primal, f32[8,128,128]{2,1,0:T(8,128)} %get-tuple-element.5.dual), custom_call_target="tpu_custom_call" | custom-call | tf_op jit(solution)/shard_map/pallas_call | solution.py:549
